TPU v7x, 32 devices: a whole 2x2x4 slice. The times are simulated.
32 devices in a mesh: windows: 2 (over x), tiles: 16 (over z, y, core).
Axes of the slice: x: 2, y: 2, z: 4, core: 2. Of those that a mesh axis runs over, the one named last changes fastest.
Arguments:
- data: bfloat16 [16, 2, 2048, 128], P('windows', None, 'tiles'), parts along dimension 0, may hold values from -6 to 6
- wavelet: float32 [8, 2], replicated, may hold values from -4 to 4
- panel_block: int32 [1], replicated, may hold values from 0 to 15
- tiles: bfloat16 [512, 2, 128, 128], P(('windows', 'tiles')), parts along dimension 0, may hold values from -0.25 to 0.25
- cover_rows: int32 [512], P(('windows', 'tiles')), parts along dimension 0, may hold values from 0 to 15, as said below
- cover_freqs: int32 [512], P(('windows', 'tiles')), parts along dimension 0, may hold values from 0 to 7
Outputs:
- residual: float32 [16, 2, 2048, 128], P('windows', None, 'tiles'), parts along dimension 0
- gradient: bfloat16 [512, 2, 128, 128], P(('windows', 'tiles')), parts along dimension 0
There are 2 independent parts, one for each index of `windows`. A program takes and returns all parts, laid end to end along the dimension named above; an argument that names none is the same for every part. Nothing has to cross between parts.
Inputs may be any that keep to these rules, and one draw needn't show every extreme that they name: `cover_rows`: among the 16 entries of one column block no row block appears more than 2 times, exactly 12 distinct row blocks appear, one row block appears 2 times in every column block, and together with cover_freqs the entries of one column block name distinct (row block, frequency) pairs.
All inputs are finite; a program needn't handle non-finite values.
Results may differ from a plain program's by a relative error of at most 0.0053.
Values may be sent and summed in bfloat16 or wider, within the bound.
No kernel may reach another device: no remote copies, remote signals or barrier semaphores. Data moves between devices by JAX's collectives and lax.ppermute only.
A program may use at most 128 MiB of HBM per device.

v0:
```python
import functools

import jax
import jax.numpy as jnp
from jax import lax
from jax.experimental import pallas as pl
from jax.experimental.pallas import tpu as pltpu
from jax.sharding import PartitionSpec as P

GROUP = 8
TABLE = 16
CHIPS = (2, 4, 6)
BF16 = jnp.bfloat16
F32 = jnp.float32
VMEM = pl.BlockSpec(memory_space=pltpu.VMEM)
SMEM = pl.BlockSpec(memory_space=pltpu.SMEM)
HBM = pl.BlockSpec(memory_space=pltpu.HBM)
ANY = pl.BlockSpec(memory_space=pl.ANY)


def call(kernel, name, out_shape, in_specs, scratch=(), out_specs=None, mib=24):
    return pl.pallas_call(
        kernel,
        name=name,
        out_shape=out_shape,
        in_specs=in_specs,
        out_specs=out_specs or jax.tree.map(lambda _: VMEM, out_shape),
        scratch_shapes=list(scratch),
        cost_estimate=pl.CostEstimate(flops=0, bytes_accessed=1 << 20, transcendentals=0),
        compiler_params=pltpu.CompilerParams(vmem_limit_bytes=mib * 1024 * 1024),
    )


def stay(array):
    return pltpu.with_memory_space_constraint(array, pltpu.HBM)


def in_hbm(shape):
    return pltpu.HBM(shape.shape, shape.dtype)


def local_index():
    return lax.rem(lax.axis_index("tiles"), GROUP)


def group_index():
    return lax.div(lax.axis_index("tiles"), GROUP)


def put(buffer, slot, count, real, imag):
    piece = real.shape[0] // GROUP
    for j in range(GROUP):
        at = slice(j * piece, (j + 1) * piece)
        first = 2 * j * piece * count + slot
        buffer[pl.ds(first, piece, stride=count), :] = real[at]
        buffer[pl.ds(first + piece * count, piece, stride=count), :] = imag[at]


def transposed_dot(left, right):
    return lax.dot_general(left, right, (((0,), (0,)), ((), ())), preferred_element_type=F32)


def member_rows(k, count):
    return pl.ds(pl.multiple_of((local_index() ^ k) * count, count), count)


def parts_kernel(data_hbm, wavelet_hbm, panel_hbm, tiles_hbm, rows_hbm, freqs_hbm, *refs):
    source, own_hbm, freqs_out, outs = *refs[:3], refs[3 : 3 + GROUP]
    data, wavelet, panel, tiles, rows, freqs, sems, wide, own = refs[3 + GROUP :]
    freq_count, _, block, shots = data.shape
    slots = tiles.shape[0]
    size = 2 * block // GROUP * slots
    half = lax.axis_size("tiles") * freq_count // 2
    pairs = (
        (data_hbm, data),
        (tiles_hbm, tiles),
        (wavelet_hbm, wavelet),
        (panel_hbm, panel),
        (freqs_hbm, freqs),
        (rows_hbm, rows),
    )
    copies = [pltpu.make_async_copy(*pair, sems.at[i]) for i, pair in enumerate(pairs)]
    for copy in copies:
        copy.start()
    diagonal = (
        lax.broadcasted_iota(jnp.int32, (block, shots), 0)
        == lax.broadcasted_iota(jnp.int32, (block, shots), 1)
    ).astype(F32)
    for i in (2, 3, 4, 5, 0):
        copies[i].wait()
    identity = diagonal * (lax.axis_index("tiles") == panel[0]).astype(F32)
    for f in range(freq_count):
        source[f, 0] = (wavelet[0, f] * identity - data[f, 0].astype(F32)).astype(BF16)
        source[f, 1] = (wavelet[1, f] * identity - data[f, 1].astype(F32)).astype(BF16)
    piece = block // GROUP
    mine = pl.ds(pl.multiple_of(local_index() * piece, piece), piece)
    for f in range(freq_count):
        for x in range(2):
            at = pl.ds(x * piece * freq_count + f, piece, stride=freq_count)
            wide[at, :] = data[f, x, mine, :].astype(F32)
    own[...] = wide[: own.shape[0]].astype(BF16)
    own_copy = pltpu.make_async_copy(own, own_hbm, sems.at[6])
    own_copy.start()
    line = lax.broadcasted_iota(jnp.int32, (slots, shots), 0)
    targets = jnp.zeros((slots, shots), jnp.int32)
    for t in range(slots):
        freqs_out[t] = freqs[t]
        targets = jnp.where(line == t, rows[t] * freq_count + freqs[t] - half, targets)
    for k in range(GROUP):
        outs[k][size:] = targets.astype(F32).astype(BF16)
    copies[1].wait()

    def one(t, carry):
        f = freqs[t]
        left = tiles[t].reshape(2 * block, block)
        right = jnp.concatenate([source[f, 0], source[f, 1]], axis=1)
        product = jnp.dot(left, right, preferred_element_type=F32)
        real = product[:block, :shots] - product[block:, shots:]
        put(wide, t, slots, real, product[:block, shots:] + product[block:, :shots])
        return carry

    lax.fori_loop(0, slots, one, 0, unroll=16)
    for k in range(GROUP):
        outs[k][:size] = wide[member_rows(k, size)].astype(BF16)
    own_copy.wait()


def sums_kernel(sizes, *refs):
    slots, groups, span, cap = sizes
    parts, (hot_out, own, *sends) = refs[:GROUP], refs[GROUP:]
    height, _, shots = own.shape
    count = GROUP * slots
    group = group_index()
    targets = jnp.concatenate([part[height * slots :] for part in parts], axis=0).astype(F32)
    lane = lax.broadcasted_iota(jnp.int32, (count, shots), 1)
    hot = []
    for q in range(0, groups, shots // span):
        here = jnp.zeros((count, shots), jnp.int32)
        for i in range(shots // span):
            inside = lane - i * span + (group ^ (q + i)) * span - groups * span // 2
            here = jnp.where(lane >= i * span, inside, here)
        hot.append((targets == here.astype(F32)).astype(F32).astype(BF16))
    if groups == 2:
        other = hot[0][:, span:]
        used = (transposed_dot(other, jnp.ones((count, shots), BF16)) > 0).astype(F32)
        before = (
            lax.broadcasted_iota(jnp.int32, (span, span), 0)
            > lax.broadcasted_iota(jnp.int32, (span, span), 1)
        ).astype(F32)
        rank = jnp.dot(before.astype(BF16), used.astype(BF16), preferred_element_type=F32)
        slot = lax.broadcasted_iota(jnp.int32, (span, shots), 1).astype(F32)
        chosen = jnp.where(rank == slot, used, 0.0)
        number = jnp.sum(used, axis=0, keepdims=True)
        target = lax.broadcasted_iota(jnp.int32, (span, shots), 0).astype(F32) + 1.0
        listed = jnp.sum(chosen * target, axis=0, keepdims=True)
        listed = jnp.where(slot[:TABLE] < span, listed, number)
        sends[0][height * cap :] = listed.astype(BF16)
        moved = jnp.dot(other, chosen[:, :span].astype(BF16), preferred_element_type=F32)
        hot = [jnp.concatenate([hot[0][:, :span], moved.astype(BF16)], axis=1)]
    hot = jnp.concatenate(hot, axis=1) if len(hot) > 1 else hot[0]
    hot_out[...] = hot
    step = 4
    for r in range(0, height, step):
        rows = [
            jnp.concatenate([part[(r + i) * slots : (r + i + 1) * slots] for part in parts], axis=0)
            for i in range(step)
        ]
        total = transposed_dot(hot, jnp.concatenate(rows, axis=1))
        for i in range(step):
            values = total[:, i * shots : (i + 1) * shots]
            own[r + i] = values[:span]
            if groups == 2:
                at = slice((r + i) * cap, (r + i + 1) * cap)
                sends[0][at] = values[span : span + cap].astype(BF16)
                sends[1][r + i] = values[span + cap :].astype(BF16)
            else:
                for q, send in enumerate(sends, 1):
                    send[r + i] = values[q * span : (q + 1) * span].astype(BF16)


def hand_out(outs, rows):
    size = outs[0].shape[0]
    outs[0][...] = rows(0)
    outs[1][...] = rows(1)
    for out, k in zip(outs[2:], CHIPS):
        out[:size] = rows(k)
        out[size:] = rows(k ^ 1)


def collect(refs, rows):
    own, *got, mate = refs
    size = own.shape[0]
    rows(0, own[...])
    rows(1, mate[:size])
    for i, k in enumerate(CHIPS):
        rows(k, got[i][:size])
        rows(k ^ 1, mate[(i + 1) * size : (i + 2) * size])


def relay_kernel(own, *refs):
    got, out = refs[:-1], refs[-1]
    size = own.shape[0]
    out[:size] = own[...]
    for i, ref in enumerate(got, 1):
        out[i * size : (i + 1) * size] = ref[size:]


def most_kernel(got, mine, *refs):
    out = refs[-1]
    last = slice(got.shape[0] - TABLE, got.shape[0])
    half = got.shape[1] // 2
    most = jnp.maximum(got[last, half:].astype(F32), mine[last, half:].astype(F32))
    out[0] = jnp.max(most).astype(jnp.int32)


def slices_kernel(data, _, *refs):
    *refs, wide, sems = refs
    count = (len(refs) - GROUP + 1) // 2
    waiting, stored, outs = refs[:count], refs[count : 2 * count], refs[2 * count :]
    copies = [
        pltpu.make_async_copy(src, dst, sems.at[i])
        for i, (src, dst) in enumerate(zip(waiting, stored))
    ]
    for copy in copies:
        copy.start()
    freq_count = data.shape[0]
    for f in range(freq_count):
        put(wide, f, freq_count, data[f, 0].astype(F32), data[f, 1].astype(F32))
    for k, out in enumerate(outs, 1):
        out[...] = wide[member_rows(k, out.shape[0])].astype(BF16)
    for copy in copies:
        copy.wait()


def fetch_rest(full, got_rest_any, got_rest, sem):
    @pl.when(full)
    def _():
        copy = pltpu.make_async_copy(got_rest_any, got_rest, sem)
        copy.start()
        copy.wait()

    @pl.when(jnp.logical_not(full))
    def _():
        got_rest[...] = jnp.zeros_like(got_rest)


def residual_kernel(sizes, own, *refs):
    slots, groups, span, cap = sizes
    height, _, shots = own.shape
    data_in, refs = refs[:GROUP], refs[GROUP:]
    if groups == 2:
        most, got, got_rest_any, rounded, send, rest_hbm, *outs = refs[:-6]
        data, back, total, sems, got_rest, rest = refs[-6:]
        target = lax.broadcasted_iota(jnp.int32, (span, span), 0).astype(F32) + 1.0
        listed = got[height * cap :, :span].astype(F32)[:1]
        chosen = (listed == target).astype(F32).astype(BF16)
        full = most[0] > cap
    else:
        got, (rounded, *outs, data, back, total, sems) = refs[: groups - 1], refs[groups - 1 :]
    local = local_index()
    freq_count = data.shape[1] // height
    own_copy = pltpu.make_async_copy(data_in[0], data.at[local], sems.at[0])
    own_copy.start()
    if groups == 2:

        fetch_rest(full, got_rest_any, got_rest, sems.at[1])
    for k in range(1, GROUP):
        data[local ^ k] = data_in[k][...]
    step = 8
    for r in range(0, height, step):
        rows = range(r, r + step)
        values = jnp.concatenate([own[i] for i in rows], axis=1)
        if groups == 2:
            more = []
            for i in rows:
                used = got[i * cap : (i + 1) * cap]
                more.append(jnp.concatenate([used, got_rest[i]], axis=0))
            more = jnp.concatenate(more, axis=1)
            values += jnp.dot(chosen, more, preferred_element_type=F32)
        else:
            for ref in got:
                values += jnp.concatenate([ref[i].astype(F32) for i in rows], axis=1)
        total[:, r * shots : (r + step) * shots] = values
        for j in range(GROUP):
            at = slice(j * freq_count, (j + 1) * freq_count)
            pair = [values[at, i * shots : (i + 1) * shots] for i in range(step)]
            pair = jnp.concatenate(pair, axis=0)
            back[j, r * freq_count : (r + step) * freq_count] = pair.astype(BF16)
    own_copy.wait()
    for r in range(0, height, step):
        rows = range(r, r + step)
        values = data[:, r * freq_count : (r + step) * freq_count].astype(F32)
        values = [
            values[:, i * freq_count : (i + 1) * freq_count].reshape(span, shots)
            for i in range(step)
        ]
        values = jnp.concatenate(values, axis=1) - total[:, r * shots : (r + step) * shots]
        values = values.astype(BF16)
        picked = transposed_dot(chosen, values).astype(BF16) if groups == 2 else None
        for i in rows:
            at = slice((i - r) * shots, (i - r + 1) * shots)
            rounded[i] = values[:, at]
            if groups == 2:
                send[i * cap : (i + 1) * cap] = picked[:cap, at]
                rest[i] = picked[cap:, at]
    if groups == 2:

        @pl.when(full)
        def _():
            copy = pltpu.make_async_copy(rest, rest_hbm, sems.at[1])
            copy.start()
            copy.wait()

    hand_out(outs, lambda k: back[local ^ k])


def spread_kernel(sizes, hot, rounded, *refs):
    slots, groups, span, cap = sizes
    height, _, shots = rounded.shape
    if groups == 2:
        most, got, got_rest_any, *outs, got_rest, sem = refs
        fetch_rest(most[0] > cap, got_rest_any, got_rest, sem)
    else:
        got, outs = refs[: groups - 1], refs[groups - 1 :]
    step = 8
    for r in range(0, height, step):
        rows = []
        for i in range(r, r + step):
            if groups == 2:
                row = [rounded[i], got[i * cap : (i + 1) * cap], got_rest[i]]
            else:
                row = [rounded[i]] + [ref[i] for ref in got]
            rows.append(jnp.concatenate(row, axis=0))
        picked = jnp.dot(hot[...], jnp.concatenate(rows, axis=1), preferred_element_type=F32)
        picked = picked.astype(BF16)
        for i in range(step):
            for k in range(GROUP):
                outs[k][(r + i) * slots : (r + i + 1) * slots] = picked[
                    k * slots : (k + 1) * slots, i * shots : (i + 1) * shots
                ]


def residual_out_kernel(data, *refs):
    back, (residual, wide) = refs[:-2], refs[-2:]
    freq_count, _, block, _ = data.shape
    size = back[0].shape[0]
    piece = block // GROUP

    def keep(k, rows):
        wide[member_rows(k, size)] = rows.astype(F32)

    collect(back, keep)
    for f in range(freq_count):
        real, imag = data[f, 0].astype(F32), data[f, 1].astype(F32)
        for j in range(GROUP):
            at = slice(j * piece, (j + 1) * piece)
            first = j * size + f
            rows = pl.ds(first, piece, stride=freq_count)
            residual[f, 0, at, :] = real[at] - wide[rows, :]
            rows = pl.ds(first + piece * freq_count, piece, stride=freq_count)
            residual[f, 1, at, :] = imag[at] - wide[rows, :]


def gradient_kernel(source, freqs, *refs):
    parts, (gradient_hbm, gradient, wide, sems) = refs[:GROUP], refs[GROUP:]
    slots, _, block, _ = gradient.shape
    size, shots = parts[0].shape
    height = size // slots
    piece = height // 2
    scale = 1.0 / shots
    for k in range(GROUP):
        wide[member_rows(k, size)] = parts[k][...].astype(F32)

    def one(t, carry):
        left = wide[pl.ds(t, GROUP * height, stride=slots), :].astype(BF16)
        right = source[freqs[t]].reshape(2 * block, shots)
        total = -scale * lax.dot_general(
            left, right, (((1,), (1,)), ((), ())), preferred_element_type=F32
        )
        real, imag = [], []
        for j in range(GROUP):
            upper = total[j * height : j * height + piece]
            lower = total[j * height + piece : (j + 1) * height]
            real.append(upper[:, :block] + lower[:, block:])
            imag.append(lower[:, :block] - upper[:, block:])
        gradient[t, 0] = jnp.concatenate(real, axis=0).astype(BF16)
        gradient[t, 1] = jnp.concatenate(imag, axis=0).astype(BF16)
        return carry

    copies = []
    quarters = 4
    step = slots // quarters
    for i in range(quarters):
        lax.fori_loop(i * step, (i + 1) * step, one, 0, unroll=4)
        at = pl.ds(i * step, step)
        copies.append(
            pltpu.make_async_copy(gradient.at[at], gradient_hbm.at[at], sems.at[i])
        )
        copies[-1].start()
    for copy in copies:
        copy.wait()


def per_device(data, wavelet, panel_block, tiles, cover_rows, cover_freqs):
    freq_count, _, block, shots = data.shape
    slots = tiles.shape[0]
    peers = lax.axis_size("tiles")
    groups = peers // GROUP
    height = 2 * block // GROUP
    span = GROUP * freq_count
    cap = 3 * span // 4 if groups == 2 else span
    sizes = (slots, groups, span, cap)

    def shape(*dims, kind=BF16):
        return jax.ShapeDtypeStruct((*dims, shots), kind)

    wide = pltpu.VMEM((GROUP * height * slots, shots), F32)
    wide_data = pltpu.VMEM((GROUP * height * freq_count, shots), F32)
    to_members = [jax.ShapeDtypeStruct((height * slots, shots), BF16)] * GROUP
    size = height * freq_count
    to_owners = [shape(size)] * 2 + [shape(2 * size)] * len(CHIPS)
    members = pltpu.VMEM((GROUP, height * freq_count, shots), BF16)

    def swap(value, distance):
        return lax.ppermute(value, "tiles", [(i, i ^ distance) for i in range(peers)])

    def in_group(values):
        got = {k: swap(values[k], k) for k in (6, 4, 2, 7, 5, 3, 1)}
        return [values[0]] + [got[k] for k in range(1, GROUP)]

    def hand_around(values):
        got = [swap(value, k) for value, k in zip(values[2:], CHIPS)]
        mate = call(relay_kernel, "for_mate", shape(4 * size), [VMEM] * (1 + len(CHIPS)))(
            values[1], *got
        )
        return [values[0], *got, swap(mate, 1)]

    def across(values):
        return [swap(value, q * GROUP) for q, value in enumerate(values, 1)]

    source, own_data, freqs, *sent = call(
        parts_kernel,
        "parts",
        [shape(freq_count, 2, block), in_hbm(shape(size)), pltpu.SMEM((slots,), jnp.int32)]
        + [shape(height * slots + slots)] * GROUP,
        [HBM] * 6,
        out_specs=[VMEM, HBM, SMEM] + [VMEM] * GROUP,
        scratch=[
            pltpu.VMEM(data.shape, BF16),
            pltpu.SMEM((2, freq_count), F32),
            pltpu.SMEM((1,), jnp.int32),
            pltpu.VMEM(tiles.shape, BF16),
            pltpu.SMEM((slots,), jnp.int32),
            pltpu.SMEM((slots,), jnp.int32),
            pltpu.SemaphoreType.DMA((7,)),
            wide,
            pltpu.VMEM((size, shots), BF16),
        ],
    )(stay(data), stay(wavelet.T), panel_block, *map(stay, (tiles, cover_rows, cover_freqs)))
    rests = [in_hbm(shape(height, span - cap))] if groups == 2 else []
    rest_rows = [pltpu.VMEM((height, span - cap, shots), BF16)] * len(rests)
    if groups == 2:
        sends = [shape(height * cap + TABLE)]
    else:
        sends = [shape(height, span)] * (groups - 1)
    hot, own, *out = call(
        functools.partial(sums_kernel, sizes),
        "sums",
        [
            jax.ShapeDtypeStruct((GROUP * slots, groups * span), BF16),
            shape(height, span, kind=F32),
        ]
        + sends
        + [shape(height, span - cap)] * len(rests),
        [VMEM] * GROUP,
    )(*in_group(sent))
    got = [swap(out[0], GROUP)] if groups == 2 else across(out)
    waiting = [hot, *out[1:]] if groups == 2 else [hot]
    stored = call(
        slices_kernel,
        "data_slices",
        [in_hbm(x) for x in waiting] + [shape(size)] * (GROUP - 1),
        [VMEM, ANY] + [VMEM] * len(waiting),
        out_specs=[HBM] * len(waiting) + [VMEM] * (GROUP - 1),
        scratch=[wide_data, pltpu.SemaphoreType.DMA((2,))],
    )(data, own, *waiting)
    hot = stored[0]
    data_in = in_group([own_data, *stored[len(waiting) :]])
    if groups == 2:
        most = call(
            most_kernel,
            "most",
            pltpu.SMEM((1,), jnp.int32),
            [VMEM] * 2 + [ANY] * (GROUP - 1),
            out_specs=SMEM,
        )(got[0], out[0], *data_in[1:])
        full = most[0] > cap

        def rest(value):
            return lax.cond(full, lambda v: swap(v, GROUP), jnp.zeros_like, value)

        got = [most, *got, rest(stored[1])]
    rounded, *out = call(
        functools.partial(residual_kernel, sizes),
        "residual_slices",
        [shape(height, span)] + [shape(height * cap)] * len(rests) + rests + to_owners,
        [VMEM, HBM]
        + [VMEM] * (GROUP - 1)
        + ([SMEM, VMEM, ANY] if groups == 2 else [VMEM] * len(got)),
        out_specs=[VMEM] * (1 + len(rests)) + [HBM] * len(rests) + [VMEM] * len(to_owners),
        scratch=[
            members,
            members,
            pltpu.VMEM((span, height * shots), F32),
            pltpu.SemaphoreType.DMA((2,)),
        ]
        + rest_rows * 2,
    )(own, stay(data_in[0]), *data_in[1:], *got)
    if groups == 2:
        got = [most, swap(out[0], GROUP), rest(out[1])]
    else:
        got = across([rounded] * (groups - 1))
    residual = call(
        residual_out_kernel,
        "residual",
        jax.ShapeDtypeStruct(data.shape, F32),
        [VMEM] * (1 + len(to_owners)),
        scratch=[wide_data],
    )(data, *hand_around(out[-len(to_owners) :]))
    out = call(
        functools.partial(spread_kernel, sizes),
        "spread",
        to_members,
        [VMEM] * 2 + ([SMEM, VMEM, ANY] if groups == 2 else [VMEM] * len(got)),
        scratch=rest_rows + [pltpu.SemaphoreType.DMA] * len(rests),
    )(hot, rounded, *got)
    gradient = call(
        gradient_kernel,
        "gradient",
        jax.ShapeDtypeStruct(tiles.shape, BF16),
        [VMEM, SMEM] + [VMEM] * GROUP,
        out_specs=HBM,
        scratch=[
            pltpu.VMEM(tiles.shape, BF16),
            wide,
            pltpu.SemaphoreType.DMA((4,)),
        ],
    )(source, freqs, *in_group(out))
    return residual, gradient


def solution(mesh):
    in_specs = (
        P("windows", None, "tiles", None),
        P(),
        P(),
        P(("windows", "tiles"), None, None, None),
        P(("windows", "tiles")),
        P(("windows", "tiles")),
    )
    out_specs = (P("windows", None, "tiles", None), P(("windows", "tiles"), None, None, None))
    return jax.shard_map(
        per_device, mesh=mesh, in_specs=in_specs, out_specs=out_specs, check_vma=False
    )
```

profile of v0, /device:TPU:0, one launch (start us, length us, event | category | flops | bytes accessed | tf_op | source)
XLA Modules:
  0.0 86.3 jit_solution(8687152084645154369)
XLA Ops:
  1.3 2.7 %parts.1 = (bf16[8,2,128,128]{3,2,1,0:T(8,128)(2,1)S(1)}, bf16[256,128]{1,0:T(8,128)(2,1)}, s32[16]{0:T(128)S(4)}, bf16[528,128]{1,0:T(8,128)(2,1)S(1)}, bf16[52...) custom-call(bf16[8,2,128,128]{3,2,1,0:T(8,128)(2,1)} %data.3, ...), custom_call_target="tpu_custom_call" | custom-call | bytes 1048576 | tf_op jit(solution)/shard_map/parts/pallas_call | solution.py:441
  4.5 2.6 %collective-permute-start.3 = (bf16[528,128]{1,0:T(8,128)(2,1)S(1)}, bf16[528,128]{1,0:T(8,128)(2,1)S(1)}, u32[]{:S(2)}, u32[]{:S(2)}) collective-permute-start(bf16[528,128]{1,0:T(8,128)(2,1)S(1)} %get-tuple-element.52), channel_id=1, source_target_pairs={{0,2},{1,3},{2,0},{3,1},{4,6},{5,7},{6,4},{7,5},{8,10},{9,11},{10,... | collective-permute-start | bytes 405512 | tf_op jit(solution)/shard_map/ppermute | solution.py:425
  7.1 1.8 %collective-permute-start.5 = (bf16[528,128]{1,0:T(8,128)(2,1)S(1)}, bf16[528,128]{1,0:T(8,128)(2,1)S(1)}, u32[]{:S(2)}, u32[]{:S(2)}) collective-permute-start(bf16[528,128]{1,0:T(8,128)(2,1)S(1)} %get-tuple-element.54), channel_id=1, source_target_pairs={{0,4},{1,5},{2,6},{3,7},{4,0},{5,1},{6,2},{7,3},{8,12},{9,13},{10,... | collective-permute-start | bytes 405512 | tf_op jit(solution)/shard_map/ppermute | solution.py:425
  8.9 2.6 %collective-permute-start.7 = (bf16[528,128]{1,0:T(8,128)(2,1)S(1)}, bf16[528,128]{1,0:T(8,128)(2,1)S(1)}, u32[]{:S(2)}, u32[]{:S(2)}) collective-permute-start(bf16[528,128]{1,0:T(8,128)(2,1)S(1)} %get-tuple-element.56), channel_id=1, source_target_pairs={{0,6},{1,7},{2,4},{3,5},{4,2},{5,3},{6,0},{7,1},{8,14},{9,15},{10,... | collective-permute-start | bytes 405512 | tf_op jit(solution)/shard_map/ppermute | solution.py:425
  11.6 1.7 %collective-permute-start.8 = (bf16[528,128]{1,0:T(8,128)(2,1)S(1)}, bf16[528,128]{1,0:T(8,128)(2,1)S(1)}, u32[]{:S(2)}, u32[]{:S(2)}) collective-permute-start(bf16[528,128]{1,0:T(8,128)(2,1)S(1)} %get-tuple-element.57), channel_id=1, source_target_pairs={{0,7},{1,6},{2,5},{3,4},{4,3},{5,2},{6,1},{7,0},{8,15},{9,14},{10,... | collective-permute-start | bytes 405512 | tf_op jit(solution)/shard_map/ppermute | solution.py:425
  13.9 1.9 %collective-permute-done.6.refs_5_ = bf16[528,128]{1,0:T(8,128)(2,1)S(1)} collective-permute-done((bf16[528,128]{1,0:T(8,128)(2,1)S(1)}, bf16[528,128]{1,0:T(8,128)(2,1)S(1)}, u32[]{:S(2)}, u32[]{:S(2)}) %collective-permute-start.6) | collective-permute-done | bytes 135200 | tf_op jit(solution)/shard_map/ppermute | solution.py:425
  15.7 4.7 %collective-permute-done.7.refs_6_ = bf16[528,128]{1,0:T(8,128)(2,1)S(1)} collective-permute-done((bf16[528,128]{1,0:T(8,128)(2,1)S(1)}, bf16[528,128]{1,0:T(8,128)(2,1)S(1)}, u32[]{:S(2)}, u32[]{:S(2)}) %collective-permute-start.7) | collective-permute-done | bytes 135200 | tf_op jit(solution)/shard_map/ppermute | solution.py:425
  20.5 1.8 %collective-permute-done.8.refs_7_ = bf16[528,128]{1,0:T(8,128)(2,1)S(1)} collective-permute-done((bf16[528,128]{1,0:T(8,128)(2,1)S(1)}, bf16[528,128]{1,0:T(8,128)(2,1)S(1)}, u32[]{:S(2)}, u32[]{:S(2)}) %collective-permute-start.8) | collective-permute-done | bytes 135200 | tf_op jit(solution)/shard_map/ppermute | solution.py:425
  23.3 2.7 %collective-permute-start.16 = (bf16[1552,128]{1,0:T(8,128)(2,1)S(1)}, bf16[1552,128]{1,0:T(8,128)(2,1)S(1)}, u32[]{:S(2)}, u32[]{:S(2)}) collective-permute-start(bf16[1552,128]{1,0:T(8,128)(2,1)S(1)} %get-tuple-element.69.mine), channel_id=1, source_target_pairs={{0,8},{1,9},{2,10},{3,11},{4,12},{5,13},{6,14},{7,15},{8,0},{9,1},... | collective-permute-start | bytes 1191944 | tf_op jit(solution)/shard_map/ppermute | solution.py:425
  28.6 1.6 %collective-permute-start.12 = (bf16[256,128]{1,0:T(8,128)(2,1)S(1)}, bf16[256,128]{1,0:T(8,128)(2,1)S(1)}, u32[]{:S(2)}, u32[]{:S(2)}) collective-permute-start(bf16[256,128]{1,0:T(8,128)(2,1)S(1)} %get-tuple-element.65), channel_id=1, source_target_pairs={{0,4},{1,5},{2,6},{3,7},{4,0},{5,1},{6,2},{7,3},{8,12},{9,13},{10,... | collective-permute-start | bytes 196616 | tf_op jit(solution)/shard_map/ppermute | solution.py:425
  34.0 3.0 %collective-permute-done.12.refs_3_.refs_4_ = bf16[256,128]{1,0:T(8,128)(2,1)S(1)} collective-permute-done((bf16[256,128]{1,0:T(8,128)(2,1)S(1)}, bf16[256,128]{1,0:T(8,128)(2,1)S(1)}, u32[]{:S(2)}, u32[]{:S(2)}) %collective-permute-start.12) | collective-permute-done | bytes 65568 | tf_op jit(solution)/shard_map/ppermute | solution.py:425
  38.4 6.3 %collective-permute-done.14.refs_5_.refs_6_ = bf16[256,128]{1,0:T(8,128)(2,1)S(1)} collective-permute-done((bf16[256,128]{1,0:T(8,128)(2,1)S(1)}, bf16[256,128]{1,0:T(8,128)(2,1)S(1)}, u32[]{:S(2)}, u32[]{:S(2)}) %collective-permute-start.14) | collective-permute-done | bytes 65568 | tf_op jit(solution)/shard_map/ppermute | solution.py:425
  46.0 2.0 %residual_slices.1 = (bf16[32,64,128]{2,1,0:T(8,128)(2,1)S(1)}, bf16[1536,128]{1,0:T(8,128)(2,1)}, bf16[32,16,128]{2,1,0:T(8,128)(2,1)}, bf16[256,128]{1,0:T(8,1...) custom-call(f32[32,64,128]{2,1,0:T(8,128)S(1)} %get-tuple-element.58, ...), custom_call_target="tpu_custom_call" | custom-call | bytes 1048576 | tf_op jit(solution)/shard_map/residual_slices/pallas_call | solution.py:503
  48.0 1.4 %collective-permute-start.17 = (bf16[512,128]{1,0:T(8,128)(2,1)S(1)}, bf16[512,128]{1,0:T(8,128)(2,1)S(1)}, u32[]{:S(2)}, u32[]{:S(2)}) collective-permute-start(bf16[512,128]{1,0:T(8,128)(2,1)S(1)} %get-tuple-element.72), channel_id=1, source_target_pairs={{0,2},{1,3},{2,0},{3,1},{4,6},{5,7},{6,4},{7,5},{8,10},{9,11},{10,... | collective-permute-start | bytes 393224 | tf_op jit(solution)/shard_map/ppermute | solution.py:425
  49.5 2.3 %collective-permute-start.18 = (bf16[512,128]{1,0:T(8,128)(2,1)S(1)}, bf16[512,128]{1,0:T(8,128)(2,1)S(1)}, u32[]{:S(2)}, u32[]{:S(2)}) collective-permute-start(bf16[512,128]{1,0:T(8,128)(2,1)S(1)} %get-tuple-element.73), channel_id=1, source_target_pairs={{0,4},{1,5},{2,6},{3,7},{4,0},{5,1},{6,2},{7,3},{8,12},{9,13},{10,... | collective-permute-start | bytes 393224 | tf_op jit(solution)/shard_map/ppermute | solution.py:425
  53.8 6.8 %collective-permute-done.18.refs_1_.refs_2_ = bf16[512,128]{1,0:T(8,128)(2,1)S(1)} collective-permute-done((bf16[512,128]{1,0:T(8,128)(2,1)S(1)}, bf16[512,128]{1,0:T(8,128)(2,1)S(1)}, u32[]{:S(2)}, u32[]{:S(2)}) %collective-permute-start.18) | collective-permute-done | bytes 131104 | tf_op jit(solution)/shard_map/ppermute | solution.py:425
  60.5 2.4 %collective-permute-done.19.refs_2_.refs_3_ = bf16[512,128]{1,0:T(8,128)(2,1)S(1)} collective-permute-done((bf16[512,128]{1,0:T(8,128)(2,1)S(1)}, bf16[512,128]{1,0:T(8,128)(2,1)S(1)}, u32[]{:S(2)}, u32[]{:S(2)}) %collective-permute-start.19) | collective-permute-done | bytes 131104 | tf_op jit(solution)/shard_map/ppermute | solution.py:425
  64.5 4.1 %collective-permute-done.21.refs_1_ = bf16[1536,128]{1,0:T(8,128)(2,1)S(1)} collective-permute-done((bf16[1536,128]{1,0:T(8,128)(2,1)}, bf16[1536,128]{1,0:T(8,128)(2,1)S(1)}, u32[]{:S(2)}, u32[]{:S(2)}) %collective-permute-start.21) | collective-permute-done | bytes 393248 | tf_op jit(solution)/shard_map/ppermute | solution.py:425
  71.0 1.7 %collective-permute-start.26 = (bf16[512,128]{1,0:T(8,128)(2,1)S(1)}, bf16[512,128]{1,0:T(8,128)(2,1)S(1)}, u32[]{:S(2)}, u32[]{:S(2)}) collective-permute-start(bf16[512,128]{1,0:T(8,128)(2,1)S(1)} %get-tuple-element.87), channel_id=1, source_target_pairs={{0,5},{1,4},{2,7},{3,6},{4,1},{5,0},{6,3},{7,2},{8,13},{9,12},{10,... | collective-permute-start | bytes 393224 | tf_op jit(solution)/shard_map/ppermute | solution.py:425
  73.1 2.5 %collective-permute-done.23.refs_2_ = bf16[512,128]{1,0:T(8,128)(2,1)S(1)} collective-permute-done((bf16[512,128]{1,0:T(8,128)(2,1)S(1)}, bf16[512,128]{1,0:T(8,128)(2,1)S(1)}, u32[]{:S(2)}, u32[]{:S(2)}) %collective-permute-start.23) | collective-permute-done | bytes 131104 | tf_op jit(solution)/shard_map/ppermute | solution.py:425
  77.4 1.6 %collective-permute-done.26.refs_5_ = bf16[512,128]{1,0:T(8,128)(2,1)S(1)} collective-permute-done((bf16[512,128]{1,0:T(8,128)(2,1)S(1)}, bf16[512,128]{1,0:T(8,128)(2,1)S(1)}, u32[]{:S(2)}, u32[]{:S(2)}) %collective-permute-start.26) | collective-permute-done | bytes 131104 | tf_op jit(solution)/shard_map/ppermute | solution.py:425
  79.0 3.9 %collective-permute-done.27.refs_6_ = bf16[512,128]{1,0:T(8,128)(2,1)S(1)} collective-permute-done((bf16[512,128]{1,0:T(8,128)(2,1)S(1)}, bf16[512,128]{1,0:T(8,128)(2,1)S(1)}, u32[]{:S(2)}, u32[]{:S(2)}) %collective-permute-start.27) | collective-permute-done | bytes 131104 | tf_op jit(solution)/shard_map/ppermute | solution.py:425
  82.9 1.6 %collective-permute-done.28.refs_7_ = bf16[512,128]{1,0:T(8,128)(2,1)S(1)} collective-permute-done((bf16[512,128]{1,0:T(8,128)(2,1)S(1)}, bf16[512,128]{1,0:T(8,128)(2,1)S(1)}, u32[]{:S(2)}, u32[]{:S(2)}) %collective-permute-start.28) | collective-permute-done | bytes 131104 | tf_op jit(solution)/shard_map/ppermute | solution.py:425
  84.5 1.8 %gradient.1 = bf16[16,2,128,128]{3,2,1,0:T(8,128)(2,1)} custom-call(bf16[8,2,128,128]{3,2,1,0:T(8,128)(2,1)S(1)} %get-tuple-element.76.source, s32[16]{0:T(128)S(4)} %get-tuple-element.77.freqs, bf16[512,128]{1,0:T(8,128)(2,1)S(1)} %get-tuple-element.82.refs_0_, bf16[512,128]{1,0:T(8,128)(2,1)S(1)} %collective-permute-done.22.refs_1_, ...), custom_call_target="tpu_custom_call" | custom-call | bytes 1048576 | tf_op jit(solution)/shard_map/gradient/pallas_call | solution.py:537
  (51 shorter events, 21.0 us)
Async XLA Ops:
  3.9 5.0 %collective-permute-start.2 = (bf16[528,128]{1,0:T(8,128)(2,1)S(1)}, bf16[528,128]{1,0:T(8,128)(2,1)S(1)}, u32[]{:S(2)}, u32[]{:S(2)}) collective-permute-start(bf16[528,128]{1,0:T(8,128)(2,1)S(1)} %get-tuple-element.51), channel_id=1, source_target_pairs={{0,1},{1,0},{2,3},{3,2},{4,5},{5,4},{6,7},{7,6},{8,9},{9,8},{10,11... | collective-permute-start | bytes 405512 | tf_op jit(solution)/shard_map/ppermute | solution.py:425
  4.5 7.1 %collective-permute-start.3 = (bf16[528,128]{1,0:T(8,128)(2,1)S(1)}, bf16[528,128]{1,0:T(8,128)(2,1)S(1)}, u32[]{:S(2)}, u32[]{:S(2)}) collective-permute-start(bf16[528,128]{1,0:T(8,128)(2,1)S(1)} %get-tuple-element.52), channel_id=1, source_target_pairs={{0,2},{1,3},{2,0},{3,1},{4,6},{5,7},{6,4},{7,5},{8,10},{9,11},{10,... | collective-permute-start | bytes 405512 | tf_op jit(solution)/shard_map/ppermute | solution.py:425
  7.0 6.8 %collective-permute-start.4 = (bf16[528,128]{1,0:T(8,128)(2,1)S(1)}, bf16[528,128]{1,0:T(8,128)(2,1)S(1)}, u32[]{:S(2)}, u32[]{:S(2)}) collective-permute-start(bf16[528,128]{1,0:T(8,128)(2,1)S(1)} %get-tuple-element.53), channel_id=1, source_target_pairs={{0,3},{1,2},{2,1},{3,0},{4,7},{5,6},{6,5},{7,4},{8,11},{9,10},{10,... | collective-permute-start | bytes 405512 | tf_op jit(solution)/shard_map/ppermute | solution.py:425
  7.1 6.7 %collective-permute-start.5 = (bf16[528,128]{1,0:T(8,128)(2,1)S(1)}, bf16[528,128]{1,0:T(8,128)(2,1)S(1)}, u32[]{:S(2)}, u32[]{:S(2)}) collective-permute-start(bf16[528,128]{1,0:T(8,128)(2,1)S(1)} %get-tuple-element.54), channel_id=1, source_target_pairs={{0,4},{1,5},{2,6},{3,7},{4,0},{5,1},{6,2},{7,3},{8,12},{9,13},{10,... | collective-permute-start | bytes 405512 | tf_op jit(solution)/shard_map/ppermute | solution.py:425
  8.9 6.8 %collective-permute-start.6 = (bf16[528,128]{1,0:T(8,128)(2,1)S(1)}, bf16[528,128]{1,0:T(8,128)(2,1)S(1)}, u32[]{:S(2)}, u32[]{:S(2)}) collective-permute-start(bf16[528,128]{1,0:T(8,128)(2,1)S(1)} %get-tuple-element.55), channel_id=1, source_target_pairs={{0,5},{1,4},{2,7},{3,6},{4,1},{5,0},{6,3},{7,2},{8,13},{9,12},{10,... | collective-permute-start | bytes 405512 | tf_op jit(solution)/shard_map/ppermute | solution.py:425
  8.9 11.6 %collective-permute-start.7 = (bf16[528,128]{1,0:T(8,128)(2,1)S(1)}, bf16[528,128]{1,0:T(8,128)(2,1)S(1)}, u32[]{:S(2)}, u32[]{:S(2)}) collective-permute-start(bf16[528,128]{1,0:T(8,128)(2,1)S(1)} %get-tuple-element.56), channel_id=1, source_target_pairs={{0,6},{1,7},{2,4},{3,5},{4,2},{5,3},{6,0},{7,1},{8,14},{9,15},{10,... | collective-permute-start | bytes 405512 | tf_op jit(solution)/shard_map/ppermute | solution.py:425
  11.6 10.7 %collective-permute-start.8 = (bf16[528,128]{1,0:T(8,128)(2,1)S(1)}, bf16[528,128]{1,0:T(8,128)(2,1)S(1)}, u32[]{:S(2)}, u32[]{:S(2)}) collective-permute-start(bf16[528,128]{1,0:T(8,128)(2,1)S(1)} %get-tuple-element.57), channel_id=1, source_target_pairs={{0,7},{1,6},{2,5},{3,4},{4,3},{5,2},{6,1},{7,0},{8,15},{9,14},{10,... | collective-permute-start | bytes 405512 | tf_op jit(solution)/shard_map/ppermute | solution.py:425
  23.3 21.9 %collective-permute-start.16 = (bf16[1552,128]{1,0:T(8,128)(2,1)S(1)}, bf16[1552,128]{1,0:T(8,128)(2,1)S(1)}, u32[]{:S(2)}, u32[]{:S(2)}) collective-permute-start(bf16[1552,128]{1,0:T(8,128)(2,1)S(1)} %get-tuple-element.69.mine), channel_id=1, source_target_pairs={{0,8},{1,9},{2,10},{3,11},{4,12},{5,13},{6,14},{7,15},{8,0},{9,1},... | collective-permute-start | bytes 1191944 | tf_op jit(solution)/shard_map/ppermute | solution.py:425
  27.3 5.5 %collective-permute-start.11 = (bf16[256,128]{1,0:T(8,128)(2,1)S(1)}, bf16[256,128]{1,0:T(8,128)(2,1)S(1)}, u32[]{:S(2)}, u32[]{:S(2)}) collective-permute-start(bf16[256,128]{1,0:T(8,128)(2,1)S(1)} %get-tuple-element.64), channel_id=1, source_target_pairs={{0,3},{1,2},{2,1},{3,0},{4,7},{5,6},{6,5},{7,4},{8,11},{9,10},{10,... | collective-permute-start | bytes 196616 | tf_op jit(solution)/shard_map/ppermute | solution.py:425
  28.6 8.3 %collective-permute-start.12 = (bf16[256,128]{1,0:T(8,128)(2,1)S(1)}, bf16[256,128]{1,0:T(8,128)(2,1)S(1)}, u32[]{:S(2)}, u32[]{:S(2)}) collective-permute-start(bf16[256,128]{1,0:T(8,128)(2,1)S(1)} %get-tuple-element.65), channel_id=1, source_target_pairs={{0,4},{1,5},{2,6},{3,7},{4,0},{5,1},{6,2},{7,3},{8,12},{9,13},{10,... | collective-permute-start | bytes 196616 | tf_op jit(solution)/shard_map/ppermute | solution.py:425
  30.2 8.2 %collective-permute-start.13 = (bf16[256,128]{1,0:T(8,128)(2,1)S(1)}, bf16[256,128]{1,0:T(8,128)(2,1)S(1)}, u32[]{:S(2)}, u32[]{:S(2)}) collective-permute-start(bf16[256,128]{1,0:T(8,128)(2,1)S(1)} %get-tuple-element.66), channel_id=1, source_target_pairs={{0,5},{1,4},{2,7},{3,6},{4,1},{5,0},{6,3},{7,2},{8,13},{9,12},{10,... | collective-permute-start | bytes 196616 | tf_op jit(solution)/shard_map/ppermute | solution.py:425
  31.7 12.9 %collective-permute-start.14 = (bf16[256,128]{1,0:T(8,128)(2,1)S(1)}, bf16[256,128]{1,0:T(8,128)(2,1)S(1)}, u32[]{:S(2)}, u32[]{:S(2)}) collective-permute-start(bf16[256,128]{1,0:T(8,128)(2,1)S(1)} %get-tuple-element.67), channel_id=1, source_target_pairs={{0,6},{1,7},{2,4},{3,5},{4,2},{5,3},{6,0},{7,1},{8,14},{9,15},{10,... | collective-permute-start | bytes 196616 | tf_op jit(solution)/shard_map/ppermute | solution.py:425
  32.8 12.4 %collective-permute-start.15 = (bf16[256,128]{1,0:T(8,128)(2,1)S(1)}, bf16[256,128]{1,0:T(8,128)(2,1)S(1)}, u32[]{:S(2)}, u32[]{:S(2)}) collective-permute-start(bf16[256,128]{1,0:T(8,128)(2,1)S(1)} %get-tuple-element.68), channel_id=1, source_target_pairs={{0,7},{1,6},{2,5},{3,4},{4,3},{5,2},{6,1},{7,0},{8,15},{9,14},{10,... | collective-permute-start | bytes 196616 | tf_op jit(solution)/shard_map/ppermute | solution.py:425
  48.0 20.7 %collective-permute-start.21 = (bf16[1536,128]{1,0:T(8,128)(2,1)}, bf16[1536,128]{1,0:T(8,128)(2,1)S(1)}, u32[]{:S(2)}, u32[]{:S(2)}) collective-permute-start(bf16[1536,128]{1,0:T(8,128)(2,1)} %get-tuple-element.80), channel_id=1, source_target_pairs={{0,8},{1,9},{2,10},{3,11},{4,12},{5,13},{6,14},{7,15},{8,0},{9,1},... | collective-permute-start | bytes 1179656 | tf_op jit(solution)/shard_map/ppermute | solution.py:425
  48.0 5.7 %collective-permute-start.17 = (bf16[512,128]{1,0:T(8,128)(2,1)S(1)}, bf16[512,128]{1,0:T(8,128)(2,1)S(1)}, u32[]{:S(2)}, u32[]{:S(2)}) collective-permute-start(bf16[512,128]{1,0:T(8,128)(2,1)S(1)} %get-tuple-element.72), channel_id=1, source_target_pairs={{0,2},{1,3},{2,0},{3,1},{4,6},{5,7},{6,4},{7,5},{8,10},{9,11},{10,... | collective-permute-start | bytes 393224 | tf_op jit(solution)/shard_map/ppermute | solution.py:425
  49.5 11.1 %collective-permute-start.18 = (bf16[512,128]{1,0:T(8,128)(2,1)S(1)}, bf16[512,128]{1,0:T(8,128)(2,1)S(1)}, u32[]{:S(2)}, u32[]{:S(2)}) collective-permute-start(bf16[512,128]{1,0:T(8,128)(2,1)S(1)} %get-tuple-element.73), channel_id=1, source_target_pairs={{0,4},{1,5},{2,6},{3,7},{4,0},{5,1},{6,2},{7,3},{8,12},{9,13},{10,... | collective-permute-start | bytes 393224 | tf_op jit(solution)/shard_map/ppermute | solution.py:425
  51.8 11.2 %collective-permute-start.19 = (bf16[512,128]{1,0:T(8,128)(2,1)S(1)}, bf16[512,128]{1,0:T(8,128)(2,1)S(1)}, u32[]{:S(2)}, u32[]{:S(2)}) collective-permute-start(bf16[512,128]{1,0:T(8,128)(2,1)S(1)} %get-tuple-element.74), channel_id=1, source_target_pairs={{0,6},{1,7},{2,4},{3,5},{4,2},{5,3},{6,0},{7,1},{8,14},{9,15},{10,... | collective-permute-start | bytes 393224 | tf_op jit(solution)/shard_map/ppermute | solution.py:425
  63.0 8.0 %collective-permute-start.20 = (bf16[1024,128]{1,0:T(8,128)(2,1)S(1)}, bf16[1024,128]{1,0:T(8,128)(2,1)S(1)}, u32[]{:S(2)}, u32[]{:S(2)}) collective-permute-start(bf16[1024,128]{1,0:T(8,128)(2,1)S(1)} %for_mate.1), channel_id=1, source_target_pairs={{0,1},{1,0},{2,3},{3,2},{4,5},{5,4},{6,7},{7,6},{8,9},{9,8},{10,11... | collective-permute-start | bytes 786440 | tf_op jit(solution)/shard_map/ppermute | solution.py:425
  69.2 6.3 %collective-permute-start.23 = (bf16[512,128]{1,0:T(8,128)(2,1)S(1)}, bf16[512,128]{1,0:T(8,128)(2,1)S(1)}, u32[]{:S(2)}, u32[]{:S(2)}) collective-permute-start(bf16[512,128]{1,0:T(8,128)(2,1)S(1)} %get-tuple-element.84), channel_id=1, source_target_pairs={{0,2},{1,3},{2,0},{3,1},{4,6},{5,7},{6,4},{7,5},{8,10},{9,11},{10,... | collective-permute-start | bytes 393224 | tf_op jit(solution)/shard_map/ppermute | solution.py:425
  69.7 7.7 %collective-permute-start.24 = (bf16[512,128]{1,0:T(8,128)(2,1)S(1)}, bf16[512,128]{1,0:T(8,128)(2,1)S(1)}, u32[]{:S(2)}, u32[]{:S(2)}) collective-permute-start(bf16[512,128]{1,0:T(8,128)(2,1)S(1)} %get-tuple-element.85), channel_id=1, source_target_pairs={{0,3},{1,2},{2,1},{3,0},{4,7},{5,6},{6,5},{7,4},{8,11},{9,10},{10,... | collective-permute-start | bytes 393224 | tf_op jit(solution)/shard_map/ppermute | solution.py:425
  71.0 6.4 %collective-permute-start.25 = (bf16[512,128]{1,0:T(8,128)(2,1)S(1)}, bf16[512,128]{1,0:T(8,128)(2,1)S(1)}, u32[]{:S(2)}, u32[]{:S(2)}) collective-permute-start(bf16[512,128]{1,0:T(8,128)(2,1)S(1)} %get-tuple-element.86), channel_id=1, source_target_pairs={{0,4},{1,5},{2,6},{3,7},{4,0},{5,1},{6,2},{7,3},{8,12},{9,13},{10,... | collective-permute-start | bytes 393224 | tf_op jit(solution)/shard_map/ppermute | solution.py:425
  71.0 8.0 %collective-permute-start.26 = (bf16[512,128]{1,0:T(8,128)(2,1)S(1)}, bf16[512,128]{1,0:T(8,128)(2,1)S(1)}, u32[]{:S(2)}, u32[]{:S(2)}) collective-permute-start(bf16[512,128]{1,0:T(8,128)(2,1)S(1)} %get-tuple-element.87), channel_id=1, source_target_pairs={{0,5},{1,4},{2,7},{3,6},{4,1},{5,0},{6,3},{7,2},{8,13},{9,12},{10,... | collective-permute-start | bytes 393224 | tf_op jit(solution)/shard_map/ppermute | solution.py:425
  72.7 10.2 %collective-permute-start.27 = (bf16[512,128]{1,0:T(8,128)(2,1)S(1)}, bf16[512,128]{1,0:T(8,128)(2,1)S(1)}, u32[]{:S(2)}, u32[]{:S(2)}) collective-permute-start(bf16[512,128]{1,0:T(8,128)(2,1)S(1)} %get-tuple-element.88), channel_id=1, source_target_pairs={{0,6},{1,7},{2,4},{3,5},{4,2},{5,3},{6,0},{7,1},{8,14},{9,15},{10,... | collective-permute-start | bytes 393224 | tf_op jit(solution)/shard_map/ppermute | solution.py:425
  75.5 9.0 %collective-permute-start.28 = (bf16[512,128]{1,0:T(8,128)(2,1)S(1)}, bf16[512,128]{1,0:T(8,128)(2,1)S(1)}, u32[]{:S(2)}, u32[]{:S(2)}) collective-permute-start(bf16[512,128]{1,0:T(8,128)(2,1)S(1)} %get-tuple-element.89), channel_id=1, source_target_pairs={{0,7},{1,6},{2,5},{3,4},{4,3},{5,2},{6,1},{7,0},{8,15},{9,14},{10,... | collective-permute-start | bytes 393224 | tf_op jit(solution)/shard_map/ppermute | solution.py:425
  (7 other events, 32.8 us)
where the time goes:
time: 86.5 us; the launch traced here: 86.3 us
  waiting for transfers between devices  46.2 us (53%)
  starting transfers between devices  26.6 us (31%)
  Pallas kernels  9.98 us (12%)
  local copies, waits for them, and re-layouts  2.13 us (2%)
  between operations  1.39 us (2%)
    ppermute x27, waiting for transfers between devices, swap(): lax.ppermute(value, 'tiles', [(i, i ^ distance) for i in range(peers)])  46.2 us
    ppermute x27, starting transfers between devices, swap(): lax.ppermute(value, 'tiles', [(i, i ^ distance) for i in range(peers)])  26.6 us
    pallas_call x1, Pallas kernels, per_device(): call(parts_kernel, 'parts', [shape(freq_count, 2, block), in_hbm(shape(si...  2.65 us
    pallas_call x1, Pallas kernels, per_device(): call(functools.partial(residual_kernel, sizes), 'residual_slices', [shape...  1.96 us
    pallas_call x1, Pallas kernels, per_device(): call(gradient_kernel, 'gradient', jax.ShapeDtypeStruct(tiles.shape, BF16)...  1.76 us
  transfers between devices with their start and end apart: 27, of which 18 were waited for; matrix products, arithmetic and copies ran while one was open for 1% of the time, Pallas kernels for 3%

commit v1 on v0

--- a/solution.py
+++ b/solution.py
@@ -249,8 +249,8 @@
     height, _, shots = own.shape
     data_in, refs = refs[:GROUP], refs[GROUP:]
     if groups == 2:
-        most, got, got_rest_any, rounded, send, rest_hbm, *outs = refs[:-6]
-        data, back, total, sems, got_rest, rest = refs[-6:]
+        most, got, got_rest_any, rounded, send_hbm, rest_hbm, *outs = refs[:-7]
+        data, back, total, sems, got_rest, rest, send = refs[-7:]
         target = lax.broadcasted_iota(jnp.int32, (span, span), 0).astype(F32) + 1.0
         listed = got[height * cap :, :span].astype(F32)[:1]
         chosen = (listed == target).astype(F32).astype(BF16)
@@ -287,6 +287,7 @@
             pair = jnp.concatenate(pair, axis=0)
             back[j, r * freq_count : (r + step) * freq_count] = pair.astype(BF16)
     own_copy.wait()
+    copies = []
     for r in range(0, height, step):
         rows = range(r, r + step)
         values = data[:, r * freq_count : (r + step) * freq_count].astype(F32)
@@ -303,6 +304,11 @@
             if groups == 2:
                 send[i * cap : (i + 1) * cap] = picked[:cap, at]
                 rest[i] = picked[cap:, at]
+        if groups == 2:
+            at = pl.ds(r * cap, step * cap)
+            sem = sems.at[2 + r // step]
+            copies.append(pltpu.make_async_copy(send.at[at], send_hbm.at[at], sem))
+            copies[-1].start()
     if groups == 2:
 
         @pl.when(full)
@@ -312,6 +318,8 @@
             copy.wait()
 
     hand_out(outs, lambda k: back[local ^ k])
+    for copy in copies:
+        copy.wait()
 
 
 def spread_kernel(sizes, hot, rounded, *refs):
@@ -414,8 +422,8 @@
     def shape(*dims, kind=BF16):
         return jax.ShapeDtypeStruct((*dims, shots), kind)
 
-    wide = pltpu.VMEM((GROUP * height * slots, shots), F32)
-    wide_data = pltpu.VMEM((GROUP * height * freq_count, shots), F32)
+    wide = pltpu.VMEM(((GROUP * height + 1) * slots, shots), F32)
+    wide_data = pltpu.VMEM(((GROUP * height + 1) * freq_count, shots), F32)
     to_members = [jax.ShapeDtypeStruct((height * slots, shots), BF16)] * GROUP
     size = height * freq_count
     to_owners = [shape(size)] * 2 + [shape(2 * size)] * len(CHIPS)
@@ -503,18 +511,22 @@
     rounded, *out = call(
         functools.partial(residual_kernel, sizes),
         "residual_slices",
-        [shape(height, span)] + [shape(height * cap)] * len(rests) + rests + to_owners,
+        [shape(height, span)]
+        + [in_hbm(shape(height * cap))] * len(rests)
+        + rests
+        + to_owners,
         [VMEM, HBM]
         + [VMEM] * (GROUP - 1)
         + ([SMEM, VMEM, ANY] if groups == 2 else [VMEM] * len(got)),
-        out_specs=[VMEM] * (1 + len(rests)) + [HBM] * len(rests) + [VMEM] * len(to_owners),
+        out_specs=[VMEM] + [HBM] * (2 * len(rests)) + [VMEM] * len(to_owners),
         scratch=[
             members,
             members,
             pltpu.VMEM((span, height * shots), F32),
-            pltpu.SemaphoreType.DMA((2,)),
+            pltpu.SemaphoreType.DMA((2 + height // 8,)),
         ]
-        + rest_rows * 2,
+        + rest_rows * 2
+        + [pltpu.VMEM((height * cap, shots), BF16)] * len(rests),
     )(own, stay(data_in[0]), *data_in[1:], *got)
     if groups == 2:
         got = [most, swap(out[0], GROUP), rest(out[1])]

time: 86.5 us -> 86.4 us (level)
  no operation moved by 1% of the time
where the time goes in v1:
time: 86.4 us; the launch traced here: 86.2 us
  waiting for transfers between devices  46.2 us (53%)
  starting transfers between devices  26.6 us (31%)
  Pallas kernels  9.87 us (11%)
  local copies, waits for them, and re-layouts  2.13 us (2%)
  between operations  1.39 us (2%)
    ppermute x27, waiting for transfers between devices, swap(): lax.ppermute(value, 'tiles', [(i, i ^ distance) for i in range(peers)])  46.2 us
    ppermute x27, starting transfers between devices, swap(): lax.ppermute(value, 'tiles', [(i, i ^ distance) for i in range(peers)])  26.6 us
    pallas_call x1, Pallas kernels, per_device(): call(parts_kernel, 'parts', [shape(freq_count, 2, block), in_hbm(shape(si...  2.65 us
    pallas_call x1, Pallas kernels, per_device(): call(functools.partial(residual_kernel, sizes), 'residual_slices', [shape...  1.86 us
    pallas_call x1, Pallas kernels, per_device(): call(gradient_kernel, 'gradient', jax.ShapeDtypeStruct(tiles.shape, BF16)...  1.75 us
  transfers between devices with their start and end apart: 27, of which 18 were waited for; matrix products, arithmetic and copies ran while one was open for 1% of the time, Pallas kernels for 3%

profile of v1, /device:TPU:0, one launch (start us, length us, event | category | flops | bytes accessed | tf_op | source)
XLA Modules:
  0.0 86.2 jit_solution(8586491697812194747)
XLA Ops:
  1.3 2.7 %parts.1 = (bf16[8,2,128,128]{3,2,1,0:T(8,128)(2,1)S(1)}, bf16[256,128]{1,0:T(8,128)(2,1)}, s32[16]{0:T(128)S(4)}, bf16[528,128]{1,0:T(8,128)(2,1)S(1)}, bf16[52...) custom-call(bf16[8,2,128,128]{3,2,1,0:T(8,128)(2,1)} %data.3, ...), custom_call_target="tpu_custom_call" | custom-call | bytes 1048576 | tf_op jit(solution)/shard_map/parts/pallas_call | solution.py:449
  4.5 2.6 %collective-permute-start.3 = (bf16[528,128]{1,0:T(8,128)(2,1)S(1)}, bf16[528,128]{1,0:T(8,128)(2,1)S(1)}, u32[]{:S(2)}, u32[]{:S(2)}) collective-permute-start(bf16[528,128]{1,0:T(8,128)(2,1)S(1)} %get-tuple-element.52), channel_id=1, source_target_pairs={{0,2},{1,3},{2,0},{3,1},{4,6},{5,7},{6,4},{7,5},{8,10},{9,11},{10,... | collective-permute-start | bytes 405512 | tf_op jit(solution)/shard_map/ppermute | solution.py:433
  7.1 1.8 %collective-permute-start.5 = (bf16[528,128]{1,0:T(8,128)(2,1)S(1)}, bf16[528,128]{1,0:T(8,128)(2,1)S(1)}, u32[]{:S(2)}, u32[]{:S(2)}) collective-permute-start(bf16[528,128]{1,0:T(8,128)(2,1)S(1)} %get-tuple-element.54), channel_id=1, source_target_pairs={{0,4},{1,5},{2,6},{3,7},{4,0},{5,1},{6,2},{7,3},{8,12},{9,13},{10,... | collective-permute-start | bytes 405512 | tf_op jit(solution)/shard_map/ppermute | solution.py:433
  8.9 2.6 %collective-permute-start.7 = (bf16[528,128]{1,0:T(8,128)(2,1)S(1)}, bf16[528,128]{1,0:T(8,128)(2,1)S(1)}, u32[]{:S(2)}, u32[]{:S(2)}) collective-permute-start(bf16[528,128]{1,0:T(8,128)(2,1)S(1)} %get-tuple-element.56), channel_id=1, source_target_pairs={{0,6},{1,7},{2,4},{3,5},{4,2},{5,3},{6,0},{7,1},{8,14},{9,15},{10,... | collective-permute-start | bytes 405512 | tf_op jit(solution)/shard_map/ppermute | solution.py:433
  11.6 1.7 %collective-permute-start.8 = (bf16[528,128]{1,0:T(8,128)(2,1)S(1)}, bf16[528,128]{1,0:T(8,128)(2,1)S(1)}, u32[]{:S(2)}, u32[]{:S(2)}) collective-permute-start(bf16[528,128]{1,0:T(8,128)(2,1)S(1)} %get-tuple-element.57), channel_id=1, source_target_pairs={{0,7},{1,6},{2,5},{3,4},{4,3},{5,2},{6,1},{7,0},{8,15},{9,14},{10,... | collective-permute-start | bytes 405512 | tf_op jit(solution)/shard_map/ppermute | solution.py:433
  13.9 1.9 %collective-permute-done.6.refs_5_ = bf16[528,128]{1,0:T(8,128)(2,1)S(1)} collective-permute-done((bf16[528,128]{1,0:T(8,128)(2,1)S(1)}, bf16[528,128]{1,0:T(8,128)(2,1)S(1)}, u32[]{:S(2)}, u32[]{:S(2)}) %collective-permute-start.6) | collective-permute-done | bytes 135200 | tf_op jit(solution)/shard_map/ppermute | solution.py:433
  15.7 4.7 %collective-permute-done.7.refs_6_ = bf16[528,128]{1,0:T(8,128)(2,1)S(1)} collective-permute-done((bf16[528,128]{1,0:T(8,128)(2,1)S(1)}, bf16[528,128]{1,0:T(8,128)(2,1)S(1)}, u32[]{:S(2)}, u32[]{:S(2)}) %collective-permute-start.7) | collective-permute-done | bytes 135200 | tf_op jit(solution)/shard_map/ppermute | solution.py:433
  20.5 1.8 %collective-permute-done.8.refs_7_ = bf16[528,128]{1,0:T(8,128)(2,1)S(1)} collective-permute-done((bf16[528,128]{1,0:T(8,128)(2,1)S(1)}, bf16[528,128]{1,0:T(8,128)(2,1)S(1)}, u32[]{:S(2)}, u32[]{:S(2)}) %collective-permute-start.8) | collective-permute-done | bytes 135200 | tf_op jit(solution)/shard_map/ppermute | solution.py:433
  23.3 2.7 %collective-permute-start.16 = (bf16[1552,128]{1,0:T(8,128)(2,1)S(1)}, bf16[1552,128]{1,0:T(8,128)(2,1)S(1)}, u32[]{:S(2)}, u32[]{:S(2)}) collective-permute-start(bf16[1552,128]{1,0:T(8,128)(2,1)S(1)} %get-tuple-element.69.mine), channel_id=1, source_target_pairs={{0,8},{1,9},{2,10},{3,11},{4,12},{5,13},{6,14},{7,15},{8,0},{9,1},... | collective-permute-start | bytes 1191944 | tf_op jit(solution)/shard_map/ppermute | solution.py:433
  28.6 1.6 %collective-permute-start.12 = (bf16[256,128]{1,0:T(8,128)(2,1)S(1)}, bf16[256,128]{1,0:T(8,128)(2,1)S(1)}, u32[]{:S(2)}, u32[]{:S(2)}) collective-permute-start(bf16[256,128]{1,0:T(8,128)(2,1)S(1)} %get-tuple-element.65), channel_id=1, source_target_pairs={{0,4},{1,5},{2,6},{3,7},{4,0},{5,1},{6,2},{7,3},{8,12},{9,13},{10,... | collective-permute-start | bytes 196616 | tf_op jit(solution)/shard_map/ppermute | solution.py:433
  34.0 3.0 %collective-permute-done.12.refs_3_.refs_4_ = bf16[256,128]{1,0:T(8,128)(2,1)S(1)} collective-permute-done((bf16[256,128]{1,0:T(8,128)(2,1)S(1)}, bf16[256,128]{1,0:T(8,128)(2,1)S(1)}, u32[]{:S(2)}, u32[]{:S(2)}) %collective-permute-start.12) | collective-permute-done | bytes 65568 | tf_op jit(solution)/shard_map/ppermute | solution.py:433
  38.4 6.3 %collective-permute-done.14.refs_5_.refs_6_ = bf16[256,128]{1,0:T(8,128)(2,1)S(1)} collective-permute-done((bf16[256,128]{1,0:T(8,128)(2,1)S(1)}, bf16[256,128]{1,0:T(8,128)(2,1)S(1)}, u32[]{:S(2)}, u32[]{:S(2)}) %collective-permute-start.14) | collective-permute-done | bytes 65568 | tf_op jit(solution)/shard_map/ppermute | solution.py:433
  46.0 1.9 %residual_slices.1 = (bf16[32,64,128]{2,1,0:T(8,128)(2,1)S(1)}, bf16[1536,128]{1,0:T(8,128)(2,1)}, bf16[32,16,128]{2,1,0:T(8,128)(2,1)}, bf16[256,128]{1,0:T(8,1...) custom-call(f32[32,64,128]{2,1,0:T(8,128)S(1)} %get-tuple-element.58, ...), custom_call_target="tpu_custom_call" | custom-call | bytes 1048576 | tf_op jit(solution)/shard_map/residual_slices/pallas_call | solution.py:511
  47.9 1.4 %collective-permute-start.17 = (bf16[512,128]{1,0:T(8,128)(2,1)S(1)}, bf16[512,128]{1,0:T(8,128)(2,1)S(1)}, u32[]{:S(2)}, u32[]{:S(2)}) collective-permute-start(bf16[512,128]{1,0:T(8,128)(2,1)S(1)} %get-tuple-element.72), channel_id=1, source_target_pairs={{0,2},{1,3},{2,0},{3,1},{4,6},{5,7},{6,4},{7,5},{8,10},{9,11},{10,... | collective-permute-start | bytes 393224 | tf_op jit(solution)/shard_map/ppermute | solution.py:433
  49.4 2.3 %collective-permute-start.18 = (bf16[512,128]{1,0:T(8,128)(2,1)S(1)}, bf16[512,128]{1,0:T(8,128)(2,1)S(1)}, u32[]{:S(2)}, u32[]{:S(2)}) collective-permute-start(bf16[512,128]{1,0:T(8,128)(2,1)S(1)} %get-tuple-element.73), channel_id=1, source_target_pairs={{0,4},{1,5},{2,6},{3,7},{4,0},{5,1},{6,2},{7,3},{8,12},{9,13},{10,... | collective-permute-start | bytes 393224 | tf_op jit(solution)/shard_map/ppermute | solution.py:433
  53.7 6.8 %collective-permute-done.18.refs_1_.refs_2_ = bf16[512,128]{1,0:T(8,128)(2,1)S(1)} collective-permute-done((bf16[512,128]{1,0:T(8,128)(2,1)S(1)}, bf16[512,128]{1,0:T(8,128)(2,1)S(1)}, u32[]{:S(2)}, u32[]{:S(2)}) %collective-permute-start.18) | collective-permute-done | bytes 131104 | tf_op jit(solution)/shard_map/ppermute | solution.py:433
  60.4 2.4 %collective-permute-done.19.refs_2_.refs_3_ = bf16[512,128]{1,0:T(8,128)(2,1)S(1)} collective-permute-done((bf16[512,128]{1,0:T(8,128)(2,1)S(1)}, bf16[512,128]{1,0:T(8,128)(2,1)S(1)}, u32[]{:S(2)}, u32[]{:S(2)}) %collective-permute-start.19) | collective-permute-done | bytes 131104 | tf_op jit(solution)/shard_map/ppermute | solution.py:433
  64.4 4.1 %collective-permute-done.21.refs_1_ = bf16[1536,128]{1,0:T(8,128)(2,1)S(1)} collective-permute-done((bf16[1536,128]{1,0:T(8,128)(2,1)}, bf16[1536,128]{1,0:T(8,128)(2,1)S(1)}, u32[]{:S(2)}, u32[]{:S(2)}) %collective-permute-start.21) | collective-permute-done | bytes 393248 | tf_op jit(solution)/shard_map/ppermute | solution.py:433
  70.9 1.7 %collective-permute-start.26 = (bf16[512,128]{1,0:T(8,128)(2,1)S(1)}, bf16[512,128]{1,0:T(8,128)(2,1)S(1)}, u32[]{:S(2)}, u32[]{:S(2)}) collective-permute-start(bf16[512,128]{1,0:T(8,128)(2,1)S(1)} %get-tuple-element.87), channel_id=1, source_target_pairs={{0,5},{1,4},{2,7},{3,6},{4,1},{5,0},{6,3},{7,2},{8,13},{9,12},{10,... | collective-permute-start | bytes 393224 | tf_op jit(solution)/shard_map/ppermute | solution.py:433
  73.0 2.5 %collective-permute-done.23.refs_2_ = bf16[512,128]{1,0:T(8,128)(2,1)S(1)} collective-permute-done((bf16[512,128]{1,0:T(8,128)(2,1)S(1)}, bf16[512,128]{1,0:T(8,128)(2,1)S(1)}, u32[]{:S(2)}, u32[]{:S(2)}) %collective-permute-start.23) | collective-permute-done | bytes 131104 | tf_op jit(solution)/shard_map/ppermute | solution.py:433
  77.3 1.6 %collective-permute-done.26.refs_5_ = bf16[512,128]{1,0:T(8,128)(2,1)S(1)} collective-permute-done((bf16[512,128]{1,0:T(8,128)(2,1)S(1)}, bf16[512,128]{1,0:T(8,128)(2,1)S(1)}, u32[]{:S(2)}, u32[]{:S(2)}) %collective-permute-start.26) | collective-permute-done | bytes 131104 | tf_op jit(solution)/shard_map/ppermute | solution.py:433
  78.9 3.9 %collective-permute-done.27.refs_6_ = bf16[512,128]{1,0:T(8,128)(2,1)S(1)} collective-permute-done((bf16[512,128]{1,0:T(8,128)(2,1)S(1)}, bf16[512,128]{1,0:T(8,128)(2,1)S(1)}, u32[]{:S(2)}, u32[]{:S(2)}) %collective-permute-start.27) | collective-permute-done | bytes 131104 | tf_op jit(solution)/shard_map/ppermute | solution.py:433
  82.8 1.6 %collective-permute-done.28.refs_7_ = bf16[512,128]{1,0:T(8,128)(2,1)S(1)} collective-permute-done((bf16[512,128]{1,0:T(8,128)(2,1)S(1)}, bf16[512,128]{1,0:T(8,128)(2,1)S(1)}, u32[]{:S(2)}, u32[]{:S(2)}) %collective-permute-start.28) | collective-permute-done | bytes 131104 | tf_op jit(solution)/shard_map/ppermute | solution.py:433
  84.4 1.7 %gradient.1 = bf16[16,2,128,128]{3,2,1,0:T(8,128)(2,1)} custom-call(bf16[8,2,128,128]{3,2,1,0:T(8,128)(2,1)S(1)} %get-tuple-element.76.source, s32[16]{0:T(128)S(4)} %get-tuple-element.77.freqs, bf16[512,128]{1,0:T(8,128)(2,1)S(1)} %get-tuple-element.82.refs_0_, bf16[512,128]{1,0:T(8,128)(2,1)S(1)} %collective-permute-done.22.refs_1_, ...), custom_call_target="tpu_custom_call" | custom-call | bytes 1048576 | tf_op jit(solution)/shard_map/gradient/pallas_call | solution.py:549
  (51 shorter events, 21.0 us)
Async XLA Ops:
  3.9 5.0 %collective-permute-start.2 = (bf16[528,128]{1,0:T(8,128)(2,1)S(1)}, bf16[528,128]{1,0:T(8,128)(2,1)S(1)}, u32[]{:S(2)}, u32[]{:S(2)}) collective-permute-start(bf16[528,128]{1,0:T(8,128)(2,1)S(1)} %get-tuple-element.51), channel_id=1, source_target_pairs={{0,1},{1,0},{2,3},{3,2},{4,5},{5,4},{6,7},{7,6},{8,9},{9,8},{10,11... | collective-permute-start | bytes 405512 | tf_op jit(solution)/shard_map/ppermute | solution.py:433
  4.5 7.1 %collective-permute-start.3 = (bf16[528,128]{1,0:T(8,128)(2,1)S(1)}, bf16[528,128]{1,0:T(8,128)(2,1)S(1)}, u32[]{:S(2)}, u32[]{:S(2)}) collective-permute-start(bf16[528,128]{1,0:T(8,128)(2,1)S(1)} %get-tuple-element.52), channel_id=1, source_target_pairs={{0,2},{1,3},{2,0},{3,1},{4,6},{5,7},{6,4},{7,5},{8,10},{9,11},{10,... | collective-permute-start | bytes 405512 | tf_op jit(solution)/shard_map/ppermute | solution.py:433
  7.0 6.8 %collective-permute-start.4 = (bf16[528,128]{1,0:T(8,128)(2,1)S(1)}, bf16[528,128]{1,0:T(8,128)(2,1)S(1)}, u32[]{:S(2)}, u32[]{:S(2)}) collective-permute-start(bf16[528,128]{1,0:T(8,128)(2,1)S(1)} %get-tuple-element.53), channel_id=1, source_target_pairs={{0,3},{1,2},{2,1},{3,0},{4,7},{5,6},{6,5},{7,4},{8,11},{9,10},{10,... | collective-permute-start | bytes 405512 | tf_op jit(solution)/shard_map/ppermute | solution.py:433
  7.1 6.7 %collective-permute-start.5 = (bf16[528,128]{1,0:T(8,128)(2,1)S(1)}, bf16[528,128]{1,0:T(8,128)(2,1)S(1)}, u32[]{:S(2)}, u32[]{:S(2)}) collective-permute-start(bf16[528,128]{1,0:T(8,128)(2,1)S(1)} %get-tuple-element.54), channel_id=1, source_target_pairs={{0,4},{1,5},{2,6},{3,7},{4,0},{5,1},{6,2},{7,3},{8,12},{9,13},{10,... | collective-permute-start | bytes 405512 | tf_op jit(solution)/shard_map/ppermute | solution.py:433
  8.9 6.8 %collective-permute-start.6 = (bf16[528,128]{1,0:T(8,128)(2,1)S(1)}, bf16[528,128]{1,0:T(8,128)(2,1)S(1)}, u32[]{:S(2)}, u32[]{:S(2)}) collective-permute-start(bf16[528,128]{1,0:T(8,128)(2,1)S(1)} %get-tuple-element.55), channel_id=1, source_target_pairs={{0,5},{1,4},{2,7},{3,6},{4,1},{5,0},{6,3},{7,2},{8,13},{9,12},{10,... | collective-permute-start | bytes 405512 | tf_op jit(solution)/shard_map/ppermute | solution.py:433
  8.9 11.6 %collective-permute-start.7 = (bf16[528,128]{1,0:T(8,128)(2,1)S(1)}, bf16[528,128]{1,0:T(8,128)(2,1)S(1)}, u32[]{:S(2)}, u32[]{:S(2)}) collective-permute-start(bf16[528,128]{1,0:T(8,128)(2,1)S(1)} %get-tuple-element.56), channel_id=1, source_target_pairs={{0,6},{1,7},{2,4},{3,5},{4,2},{5,3},{6,0},{7,1},{8,14},{9,15},{10,... | collective-permute-start | bytes 405512 | tf_op jit(solution)/shard_map/ppermute | solution.py:433
  11.6 10.7 %collective-permute-start.8 = (bf16[528,128]{1,0:T(8,128)(2,1)S(1)}, bf16[528,128]{1,0:T(8,128)(2,1)S(1)}, u32[]{:S(2)}, u32[]{:S(2)}) collective-permute-start(bf16[528,128]{1,0:T(8,128)(2,1)S(1)} %get-tuple-element.57), channel_id=1, source_target_pairs={{0,7},{1,6},{2,5},{3,4},{4,3},{5,2},{6,1},{7,0},{8,15},{9,14},{10,... | collective-permute-start | bytes 405512 | tf_op jit(solution)/shard_map/ppermute | solution.py:433
  23.3 21.9 %collective-permute-start.16 = (bf16[1552,128]{1,0:T(8,128)(2,1)S(1)}, bf16[1552,128]{1,0:T(8,128)(2,1)S(1)}, u32[]{:S(2)}, u32[]{:S(2)}) collective-permute-start(bf16[1552,128]{1,0:T(8,128)(2,1)S(1)} %get-tuple-element.69.mine), channel_id=1, source_target_pairs={{0,8},{1,9},{2,10},{3,11},{4,12},{5,13},{6,14},{7,15},{8,0},{9,1},... | collective-permute-start | bytes 1191944 | tf_op jit(solution)/shard_map/ppermute | solution.py:433
  27.3 5.5 %collective-permute-start.11 = (bf16[256,128]{1,0:T(8,128)(2,1)S(1)}, bf16[256,128]{1,0:T(8,128)(2,1)S(1)}, u32[]{:S(2)}, u32[]{:S(2)}) collective-permute-start(bf16[256,128]{1,0:T(8,128)(2,1)S(1)} %get-tuple-element.64), channel_id=1, source_target_pairs={{0,3},{1,2},{2,1},{3,0},{4,7},{5,6},{6,5},{7,4},{8,11},{9,10},{10,... | collective-permute-start | bytes 196616 | tf_op jit(solution)/shard_map/ppermute | solution.py:433
  28.6 8.3 %collective-permute-start.12 = (bf16[256,128]{1,0:T(8,128)(2,1)S(1)}, bf16[256,128]{1,0:T(8,128)(2,1)S(1)}, u32[]{:S(2)}, u32[]{:S(2)}) collective-permute-start(bf16[256,128]{1,0:T(8,128)(2,1)S(1)} %get-tuple-element.65), channel_id=1, source_target_pairs={{0,4},{1,5},{2,6},{3,7},{4,0},{5,1},{6,2},{7,3},{8,12},{9,13},{10,... | collective-permute-start | bytes 196616 | tf_op jit(solution)/shard_map/ppermute | solution.py:433
  30.2 8.2 %collective-permute-start.13 = (bf16[256,128]{1,0:T(8,128)(2,1)S(1)}, bf16[256,128]{1,0:T(8,128)(2,1)S(1)}, u32[]{:S(2)}, u32[]{:S(2)}) collective-permute-start(bf16[256,128]{1,0:T(8,128)(2,1)S(1)} %get-tuple-element.66), channel_id=1, source_target_pairs={{0,5},{1,4},{2,7},{3,6},{4,1},{5,0},{6,3},{7,2},{8,13},{9,12},{10,... | collective-permute-start | bytes 196616 | tf_op jit(solution)/shard_map/ppermute | solution.py:433
  31.7 12.9 %collective-permute-start.14 = (bf16[256,128]{1,0:T(8,128)(2,1)S(1)}, bf16[256,128]{1,0:T(8,128)(2,1)S(1)}, u32[]{:S(2)}, u32[]{:S(2)}) collective-permute-start(bf16[256,128]{1,0:T(8,128)(2,1)S(1)} %get-tuple-element.67), channel_id=1, source_target_pairs={{0,6},{1,7},{2,4},{3,5},{4,2},{5,3},{6,0},{7,1},{8,14},{9,15},{10,... | collective-permute-start | bytes 196616 | tf_op jit(solution)/shard_map/ppermute | solution.py:433
  32.8 12.4 %collective-permute-start.15 = (bf16[256,128]{1,0:T(8,128)(2,1)S(1)}, bf16[256,128]{1,0:T(8,128)(2,1)S(1)}, u32[]{:S(2)}, u32[]{:S(2)}) collective-permute-start(bf16[256,128]{1,0:T(8,128)(2,1)S(1)} %get-tuple-element.68), channel_id=1, source_target_pairs={{0,7},{1,6},{2,5},{3,4},{4,3},{5,2},{6,1},{7,0},{8,15},{9,14},{10,... | collective-permute-start | bytes 196616 | tf_op jit(solution)/shard_map/ppermute | solution.py:433
  47.9 20.7 %collective-permute-start.21 = (bf16[1536,128]{1,0:T(8,128)(2,1)}, bf16[1536,128]{1,0:T(8,128)(2,1)S(1)}, u32[]{:S(2)}, u32[]{:S(2)}) collective-permute-start(bf16[1536,128]{1,0:T(8,128)(2,1)} %get-tuple-element.80), channel_id=1, source_target_pairs={{0,8},{1,9},{2,10},{3,11},{4,12},{5,13},{6,14},{7,15},{8,0},{9,1},... | collective-permute-start | bytes 1179656 | tf_op jit(solution)/shard_map/ppermute | solution.py:433
  47.9 5.7 %collective-permute-start.17 = (bf16[512,128]{1,0:T(8,128)(2,1)S(1)}, bf16[512,128]{1,0:T(8,128)(2,1)S(1)}, u32[]{:S(2)}, u32[]{:S(2)}) collective-permute-start(bf16[512,128]{1,0:T(8,128)(2,1)S(1)} %get-tuple-element.72), channel_id=1, source_target_pairs={{0,2},{1,3},{2,0},{3,1},{4,6},{5,7},{6,4},{7,5},{8,10},{9,11},{10,... | collective-permute-start | bytes 393224 | tf_op jit(solution)/shard_map/ppermute | solution.py:433
  49.4 11.1 %collective-permute-start.18 = (bf16[512,128]{1,0:T(8,128)(2,1)S(1)}, bf16[512,128]{1,0:T(8,128)(2,1)S(1)}, u32[]{:S(2)}, u32[]{:S(2)}) collective-permute-start(bf16[512,128]{1,0:T(8,128)(2,1)S(1)} %get-tuple-element.73), channel_id=1, source_target_pairs={{0,4},{1,5},{2,6},{3,7},{4,0},{5,1},{6,2},{7,3},{8,12},{9,13},{10,... | collective-permute-start | bytes 393224 | tf_op jit(solution)/shard_map/ppermute | solution.py:433
  51.7 11.2 %collective-permute-start.19 = (bf16[512,128]{1,0:T(8,128)(2,1)S(1)}, bf16[512,128]{1,0:T(8,128)(2,1)S(1)}, u32[]{:S(2)}, u32[]{:S(2)}) collective-permute-start(bf16[512,128]{1,0:T(8,128)(2,1)S(1)} %get-tuple-element.74), channel_id=1, source_target_pairs={{0,6},{1,7},{2,4},{3,5},{4,2},{5,3},{6,0},{7,1},{8,14},{9,15},{10,... | collective-permute-start | bytes 393224 | tf_op jit(solution)/shard_map/ppermute | solution.py:433
  62.9 8.0 %collective-permute-start.20 = (bf16[1024,128]{1,0:T(8,128)(2,1)S(1)}, bf16[1024,128]{1,0:T(8,128)(2,1)S(1)}, u32[]{:S(2)}, u32[]{:S(2)}) collective-permute-start(bf16[1024,128]{1,0:T(8,128)(2,1)S(1)} %for_mate.1), channel_id=1, source_target_pairs={{0,1},{1,0},{2,3},{3,2},{4,5},{5,4},{6,7},{7,6},{8,9},{9,8},{10,11... | collective-permute-start | bytes 786440 | tf_op jit(solution)/shard_map/ppermute | solution.py:433
  69.1 6.3 %collective-permute-start.23 = (bf16[512,128]{1,0:T(8,128)(2,1)S(1)}, bf16[512,128]{1,0:T(8,128)(2,1)S(1)}, u32[]{:S(2)}, u32[]{:S(2)}) collective-permute-start(bf16[512,128]{1,0:T(8,128)(2,1)S(1)} %get-tuple-element.84), channel_id=1, source_target_pairs={{0,2},{1,3},{2,0},{3,1},{4,6},{5,7},{6,4},{7,5},{8,10},{9,11},{10,... | collective-permute-start | bytes 393224 | tf_op jit(solution)/shard_map/ppermute | solution.py:433
  69.6 7.7 %collective-permute-start.24 = (bf16[512,128]{1,0:T(8,128)(2,1)S(1)}, bf16[512,128]{1,0:T(8,128)(2,1)S(1)}, u32[]{:S(2)}, u32[]{:S(2)}) collective-permute-start(bf16[512,128]{1,0:T(8,128)(2,1)S(1)} %get-tuple-element.85), channel_id=1, source_target_pairs={{0,3},{1,2},{2,1},{3,0},{4,7},{5,6},{6,5},{7,4},{8,11},{9,10},{10,... | collective-permute-start | bytes 393224 | tf_op jit(solution)/shard_map/ppermute | solution.py:433
  70.9 6.4 %collective-permute-start.25 = (bf16[512,128]{1,0:T(8,128)(2,1)S(1)}, bf16[512,128]{1,0:T(8,128)(2,1)S(1)}, u32[]{:S(2)}, u32[]{:S(2)}) collective-permute-start(bf16[512,128]{1,0:T(8,128)(2,1)S(1)} %get-tuple-element.86), channel_id=1, source_target_pairs={{0,4},{1,5},{2,6},{3,7},{4,0},{5,1},{6,2},{7,3},{8,12},{9,13},{10,... | collective-permute-start | bytes 393224 | tf_op jit(solution)/shard_map/ppermute | solution.py:433
  70.9 8.0 %collective-permute-start.26 = (bf16[512,128]{1,0:T(8,128)(2,1)S(1)}, bf16[512,128]{1,0:T(8,128)(2,1)S(1)}, u32[]{:S(2)}, u32[]{:S(2)}) collective-permute-start(bf16[512,128]{1,0:T(8,128)(2,1)S(1)} %get-tuple-element.87), channel_id=1, source_target_pairs={{0,5},{1,4},{2,7},{3,6},{4,1},{5,0},{6,3},{7,2},{8,13},{9,12},{10,... | collective-permute-start | bytes 393224 | tf_op jit(solution)/shard_map/ppermute | solution.py:433
  72.6 10.2 %collective-permute-start.27 = (bf16[512,128]{1,0:T(8,128)(2,1)S(1)}, bf16[512,128]{1,0:T(8,128)(2,1)S(1)}, u32[]{:S(2)}, u32[]{:S(2)}) collective-permute-start(bf16[512,128]{1,0:T(8,128)(2,1)S(1)} %get-tuple-element.88), channel_id=1, source_target_pairs={{0,6},{1,7},{2,4},{3,5},{4,2},{5,3},{6,0},{7,1},{8,14},{9,15},{10,... | collective-permute-start | bytes 393224 | tf_op jit(solution)/shard_map/ppermute | solution.py:433
  75.4 9.0 %collective-permute-start.28 = (bf16[512,128]{1,0:T(8,128)(2,1)S(1)}, bf16[512,128]{1,0:T(8,128)(2,1)S(1)}, u32[]{:S(2)}, u32[]{:S(2)}) collective-permute-start(bf16[512,128]{1,0:T(8,128)(2,1)S(1)} %get-tuple-element.89), channel_id=1, source_target_pairs={{0,7},{1,6},{2,5},{3,4},{4,3},{5,2},{6,1},{7,0},{8,15},{9,14},{10,... | collective-permute-start | bytes 393224 | tf_op jit(solution)/shard_map/ppermute | solution.py:433
  (7 other events, 32.8 us)

commit v2 on v1

--- a/solution.py
+++ b/solution.py
@@ -65,8 +65,8 @@
 
 
 def parts_kernel(data_hbm, wavelet_hbm, panel_hbm, tiles_hbm, rows_hbm, freqs_hbm, *refs):
-    source, own_hbm, freqs_out, outs = *refs[:3], refs[3 : 3 + GROUP]
-    data, wavelet, panel, tiles, rows, freqs, sems, wide, own = refs[3 + GROUP :]
+    source_hbm, own_hbm, freqs_out, outs = *refs[:3], refs[3 : 3 + GROUP]
+    data, wavelet, panel, tiles, rows, freqs, sems, wide, own, source = refs[3 + GROUP :]
     freq_count, _, block, shots = data.shape
     slots = tiles.shape[0]
     size = 2 * block // GROUP * slots
@@ -99,8 +99,12 @@
             at = pl.ds(x * piece * freq_count + f, piece, stride=freq_count)
             wide[at, :] = data[f, x, mine, :].astype(F32)
     own[...] = wide[: own.shape[0]].astype(BF16)
-    own_copy = pltpu.make_async_copy(own, own_hbm, sems.at[6])
-    own_copy.start()
+    stores = [
+        pltpu.make_async_copy(own, own_hbm, sems.at[6]),
+        pltpu.make_async_copy(source, source_hbm, sems.at[7]),
+    ]
+    for store in stores:
+        store.start()
     line = lax.broadcasted_iota(jnp.int32, (slots, shots), 0)
     targets = jnp.zeros((slots, shots), jnp.int32)
     for t in range(slots):
@@ -122,7 +126,8 @@
     lax.fori_loop(0, slots, one, 0, unroll=16)
     for k in range(GROUP):
         outs[k][:size] = wide[member_rows(k, size)].astype(BF16)
-    own_copy.wait()
+    for store in stores:
+        store.wait()
 
 
 def sums_kernel(sizes, *refs):
@@ -215,7 +220,7 @@
 
 def slices_kernel(data, _, *refs):
     *refs, wide, sems = refs
-    count = (len(refs) - GROUP + 1) // 2
+    count = (len(refs) - 1 - len(CHIPS)) // 2
     waiting, stored, outs = refs[:count], refs[count : 2 * count], refs[2 * count :]
     copies = [
         pltpu.make_async_copy(src, dst, sems.at[i])
@@ -226,8 +231,11 @@
     freq_count = data.shape[0]
     for f in range(freq_count):
         put(wide, f, freq_count, data[f, 0].astype(F32), data[f, 1].astype(F32))
-    for k, out in enumerate(outs, 1):
-        out[...] = wide[member_rows(k, out.shape[0])].astype(BF16)
+    size = outs[0].shape[0]
+    outs[0][...] = wide[member_rows(1, size)].astype(BF16)
+    for out, k in zip(outs[1:], CHIPS):
+        out[:size] = wide[member_rows(k, size)].astype(BF16)
+        out[size:] = wide[member_rows(k ^ 1, size)].astype(BF16)
     for copy in copies:
         copy.wait()
 
@@ -247,7 +255,7 @@
 def residual_kernel(sizes, own, *refs):
     slots, groups, span, cap = sizes
     height, _, shots = own.shape
-    data_in, refs = refs[:GROUP], refs[GROUP:]
+    data_in, refs = refs[: 2 + len(CHIPS)], refs[2 + len(CHIPS) :]
     if groups == 2:
         most, got, got_rest_any, rounded, send_hbm, rest_hbm, *outs = refs[:-7]
         data, back, total, sems, got_rest, rest, send = refs[-7:]
@@ -264,8 +272,12 @@
     if groups == 2:
 
         fetch_rest(full, got_rest_any, got_rest, sems.at[1])
-    for k in range(1, GROUP):
-        data[local ^ k] = data_in[k][...]
+    *got_data, mate = data_in[1:]
+    size = mate.shape[0] // 4
+    data[local ^ 1] = mate[:size]
+    for i, k in enumerate(CHIPS):
+        data[local ^ k] = got_data[i][:size]
+        data[local ^ k ^ 1] = mate[(i + 1) * size : (i + 2) * size]
     step = 8
     for r in range(0, height, step):
         rows = range(r, r + step)
@@ -449,10 +461,10 @@
     source, own_data, freqs, *sent = call(
         parts_kernel,
         "parts",
-        [shape(freq_count, 2, block), in_hbm(shape(size)), pltpu.SMEM((slots,), jnp.int32)]
+        [in_hbm(shape(freq_count, 2, block)), in_hbm(shape(size)), pltpu.SMEM((slots,), jnp.int32)]
         + [shape(height * slots + slots)] * GROUP,
         [HBM] * 6,
-        out_specs=[VMEM, HBM, SMEM] + [VMEM] * GROUP,
+        out_specs=[HBM, HBM, SMEM] + [VMEM] * GROUP,
         scratch=[
             pltpu.VMEM(data.shape, BF16),
             pltpu.SMEM((2, freq_count), F32),
@@ -460,9 +472,10 @@
             pltpu.VMEM(tiles.shape, BF16),
             pltpu.SMEM((slots,), jnp.int32),
             pltpu.SMEM((slots,), jnp.int32),
-            pltpu.SemaphoreType.DMA((7,)),
+            pltpu.SemaphoreType.DMA((8,)),
             wide,
             pltpu.VMEM((size, shots), BF16),
+            pltpu.VMEM(data.shape, BF16),
         ],
     )(stay(data), stay(wavelet.T), panel_block, *map(stay, (tiles, cover_rows, cover_freqs)))
     rests = [in_hbm(shape(height, span - cap))] if groups == 2 else []
@@ -487,19 +500,19 @@
     stored = call(
         slices_kernel,
         "data_slices",
-        [in_hbm(x) for x in waiting] + [shape(size)] * (GROUP - 1),
+        [in_hbm(x) for x in waiting] + to_owners[1:],
         [VMEM, ANY] + [VMEM] * len(waiting),
-        out_specs=[HBM] * len(waiting) + [VMEM] * (GROUP - 1),
+        out_specs=[HBM] * len(waiting) + [VMEM] * (len(to_owners) - 1),
         scratch=[wide_data, pltpu.SemaphoreType.DMA((2,))],
     )(data, own, *waiting)
     hot = stored[0]
-    data_in = in_group([own_data, *stored[len(waiting) :]])
+    data_in = hand_around([own_data, *stored[len(waiting) :]])
     if groups == 2:
         most = call(
             most_kernel,
             "most",
             pltpu.SMEM((1,), jnp.int32),
-            [VMEM] * 2 + [ANY] * (GROUP - 1),
+            [VMEM] * 2 + [ANY] * (len(data_in) - 1),
             out_specs=SMEM,
         )(got[0], out[0], *data_in[1:])
         full = most[0] > cap
@@ -516,7 +529,7 @@
         + rests
         + to_owners,
         [VMEM, HBM]
-        + [VMEM] * (GROUP - 1)
+        + [VMEM] * (len(data_in) - 1)
         + ([SMEM, VMEM, ANY] if groups == 2 else [VMEM] * len(got)),
         out_specs=[VMEM] + [HBM] * (2 * len(rests)) + [VMEM] * len(to_owners),
         scratch=[

time: 86.4 us -> 85.2 us (0.986)
  starting transfers between devices: 26.6 us -> 25.3 us
    ppermute x27 -> x24, starting transfers between devices: 26.6 us -> 25.3 us  [swap(): lax.ppermute(value, 'tiles', [(i, i ^ distance) for i in range(peers)])]
    ppermute x27 -> x24, waiting for transfers between devices: 46.2 us -> 46.1 us  [swap(): lax.ppermute(value, 'tiles', [(i, i ^ distance) for i in range(peers)])]
  transfers between devices with their start and end apart: 27 -> 24, of which waited for: 18 -> 18; matrix products, arithmetic and copies ran while one was open for 1% -> 1% of each run, Pallas kernels for 3% -> 3%
where the time goes in v2:
time: 85.2 us; the launch traced here: 84.9 us
  waiting for transfers between devices  46.1 us (54%)
  starting transfers between devices  25.3 us (30%)
  Pallas kernels  9.91 us (12%)
  local copies, waits for them, and re-layouts  2.15 us (3%)
  between operations  1.4 us (2%)
    ppermute x24, waiting for transfers between devices, swap(): lax.ppermute(value, 'tiles', [(i, i ^ distance) for i in range(peers)])  46.1 us
    ppermute x24, starting transfers between devices, swap(): lax.ppermute(value, 'tiles', [(i, i ^ distance) for i in range(peers)])  25.3 us
    pallas_call x1, Pallas kernels, per_device(): call(parts_kernel, 'parts', [in_hbm(shape(freq_count, 2, block)), in_hbm(...  2.67 us
    pallas_call x1, Pallas kernels, per_device(): call(functools.partial(residual_kernel, sizes), 'residual_slices', [shape...  1.86 us
    pallas_call x1, Pallas kernels, per_device(): call(gradient_kernel, 'gradient', jax.ShapeDtypeStruct(tiles.shape, BF16)...  1.76 us
  transfers between devices with their start and end apart: 24, of which 18 were waited for; matrix products, arithmetic and copies ran while one was open for 1% of the time, Pallas kernels for 3%

profile of v2, /device:TPU:0, one launch (start us, length us, event | category | flops | bytes accessed | tf_op | source)
XLA Modules:
  0.0 84.9 jit_solution(4812458674796282975)
XLA Ops:
  1.3 2.7 %parts.1 = (bf16[8,2,128,128]{3,2,1,0:T(8,128)(2,1)}, bf16[256,128]{1,0:T(8,128)(2,1)}, s32[16]{0:T(128)S(4)}, bf16[528,128]{1,0:T(8,128)(2,1)S(1)}, bf16[528,12...) custom-call(bf16[8,2,128,128]{3,2,1,0:T(8,128)(2,1)} %data.3, ...), custom_call_target="tpu_custom_call" | custom-call | bytes 1048576 | tf_op jit(solution)/shard_map/parts/pallas_call | solution.py:461
  4.5 2.6 %collective-permute-start.3 = (bf16[528,128]{1,0:T(8,128)(2,1)S(1)}, bf16[528,128]{1,0:T(8,128)(2,1)S(1)}, u32[]{:S(2)}, u32[]{:S(2)}) collective-permute-start(bf16[528,128]{1,0:T(8,128)(2,1)S(1)} %get-tuple-element.49), channel_id=1, source_target_pairs={{0,2},{1,3},{2,0},{3,1},{4,6},{5,7},{6,4},{7,5},{8,10},{9,11},{10,... | collective-permute-start | bytes 405512 | tf_op jit(solution)/shard_map/ppermute | solution.py:445
  7.1 1.8 %collective-permute-start.5 = (bf16[528,128]{1,0:T(8,128)(2,1)S(1)}, bf16[528,128]{1,0:T(8,128)(2,1)S(1)}, u32[]{:S(2)}, u32[]{:S(2)}) collective-permute-start(bf16[528,128]{1,0:T(8,128)(2,1)S(1)} %get-tuple-element.51), channel_id=1, source_target_pairs={{0,4},{1,5},{2,6},{3,7},{4,0},{5,1},{6,2},{7,3},{8,12},{9,13},{10,... | collective-permute-start | bytes 405512 | tf_op jit(solution)/shard_map/ppermute | solution.py:445
  8.9 2.6 %collective-permute-start.7 = (bf16[528,128]{1,0:T(8,128)(2,1)S(1)}, bf16[528,128]{1,0:T(8,128)(2,1)S(1)}, u32[]{:S(2)}, u32[]{:S(2)}) collective-permute-start(bf16[528,128]{1,0:T(8,128)(2,1)S(1)} %get-tuple-element.53), channel_id=1, source_target_pairs={{0,6},{1,7},{2,4},{3,5},{4,2},{5,3},{6,0},{7,1},{8,14},{9,15},{10,... | collective-permute-start | bytes 405512 | tf_op jit(solution)/shard_map/ppermute | solution.py:445
  11.6 1.7 %collective-permute-start.8 = (bf16[528,128]{1,0:T(8,128)(2,1)S(1)}, bf16[528,128]{1,0:T(8,128)(2,1)S(1)}, u32[]{:S(2)}, u32[]{:S(2)}) collective-permute-start(bf16[528,128]{1,0:T(8,128)(2,1)S(1)} %get-tuple-element.54), channel_id=1, source_target_pairs={{0,7},{1,6},{2,5},{3,4},{4,3},{5,2},{6,1},{7,0},{8,15},{9,14},{10,... | collective-permute-start | bytes 405512 | tf_op jit(solution)/shard_map/ppermute | solution.py:445
  13.9 1.9 %collective-permute-done.6.refs_5_ = bf16[528,128]{1,0:T(8,128)(2,1)S(1)} collective-permute-done((bf16[528,128]{1,0:T(8,128)(2,1)S(1)}, bf16[528,128]{1,0:T(8,128)(2,1)S(1)}, u32[]{:S(2)}, u32[]{:S(2)}) %collective-permute-start.6) | collective-permute-done | bytes 135200 | tf_op jit(solution)/shard_map/ppermute | solution.py:445
  15.8 4.7 %collective-permute-done.7.refs_6_ = bf16[528,128]{1,0:T(8,128)(2,1)S(1)} collective-permute-done((bf16[528,128]{1,0:T(8,128)(2,1)S(1)}, bf16[528,128]{1,0:T(8,128)(2,1)S(1)}, u32[]{:S(2)}, u32[]{:S(2)}) %collective-permute-start.7) | collective-permute-done | bytes 135200 | tf_op jit(solution)/shard_map/ppermute | solution.py:445
  20.5 1.8 %collective-permute-done.8.refs_7_ = bf16[528,128]{1,0:T(8,128)(2,1)S(1)} collective-permute-done((bf16[528,128]{1,0:T(8,128)(2,1)S(1)}, bf16[528,128]{1,0:T(8,128)(2,1)S(1)}, u32[]{:S(2)}, u32[]{:S(2)}) %collective-permute-start.8) | collective-permute-done | bytes 135200 | tf_op jit(solution)/shard_map/ppermute | solution.py:445
  23.3 2.7 %collective-permute-start.13 = (bf16[1552,128]{1,0:T(8,128)(2,1)S(1)}, bf16[1552,128]{1,0:T(8,128)(2,1)S(1)}, u32[]{:S(2)}, u32[]{:S(2)}) collective-permute-start(bf16[1552,128]{1,0:T(8,128)(2,1)S(1)} %get-tuple-element.63.mine), channel_id=1, source_target_pairs={{0,8},{1,9},{2,10},{3,11},{4,12},{5,13},{6,14},{7,15},{8,0},{9,1},... | collective-permute-start | bytes 1191944 | tf_op jit(solution)/shard_map/ppermute | solution.py:445
  27.3 1.6 %collective-permute-start.10 = (bf16[512,128]{1,0:T(8,128)(2,1)S(1)}, bf16[512,128]{1,0:T(8,128)(2,1)S(1)}, u32[]{:S(2)}, u32[]{:S(2)}) collective-permute-start(bf16[512,128]{1,0:T(8,128)(2,1)S(1)} %get-tuple-element.60), channel_id=1, source_target_pairs={{0,4},{1,5},{2,6},{3,7},{4,0},{5,1},{6,2},{7,3},{8,12},{9,13},{10,... | collective-permute-start | bytes 393224 | tf_op jit(solution)/shard_map/ppermute | solution.py:445
  30.2 2.0 %collective-permute-done.9.refs_0_.refs_1_ = bf16[512,128]{1,0:T(8,128)(2,1)S(1)} collective-permute-done((bf16[512,128]{1,0:T(8,128)(2,1)S(1)}, bf16[512,128]{1,0:T(8,128)(2,1)S(1)}, u32[]{:S(2)}, u32[]{:S(2)}) %collective-permute-start.9) | collective-permute-done | bytes 131104 | tf_op jit(solution)/shard_map/ppermute | solution.py:445
  32.2 6.1 %collective-permute-done.10.refs_1_.refs_2_ = bf16[512,128]{1,0:T(8,128)(2,1)S(1)} collective-permute-done((bf16[512,128]{1,0:T(8,128)(2,1)S(1)}, bf16[512,128]{1,0:T(8,128)(2,1)S(1)}, u32[]{:S(2)}, u32[]{:S(2)}) %collective-permute-start.10) | collective-permute-done | bytes 131104 | tf_op jit(solution)/shard_map/ppermute | solution.py:445
  38.4 2.3 %collective-permute-done.11.refs_2_.refs_3_ = bf16[512,128]{1,0:T(8,128)(2,1)S(1)} collective-permute-done((bf16[512,128]{1,0:T(8,128)(2,1)S(1)}, bf16[512,128]{1,0:T(8,128)(2,1)S(1)}, u32[]{:S(2)}, u32[]{:S(2)}) %collective-permute-start.11) | collective-permute-done | bytes 131104 | tf_op jit(solution)/shard_map/ppermute | solution.py:445
  42.3 2.0 %collective-permute-done.13.got.refs_6_ = bf16[1552,128]{1,0:T(8,128)(2,1)S(1)} collective-permute-done((bf16[1552,128]{1,0:T(8,128)(2,1)S(1)}, bf16[1552,128]{1,0:T(8,128)(2,1)S(1)}, u32[]{:S(2)}, u32[]{:S(2)}) %collective-permute-start.13) | collective-permute-done | bytes 397344 | tf_op jit(solution)/shard_map/ppermute | solution.py:445
  45.1 1.9 %residual_slices.1 = (bf16[32,64,128]{2,1,0:T(8,128)(2,1)S(1)}, bf16[1536,128]{1,0:T(8,128)(2,1)}, bf16[32,16,128]{2,1,0:T(8,128)(2,1)}, bf16[256,128]{1,0:T(8,1...) custom-call(f32[32,64,128]{2,1,0:T(8,128)S(1)} %get-tuple-element.55, ...), custom_call_target="tpu_custom_call" | custom-call | bytes 1048576 | tf_op jit(solution)/shard_map/residual_slices/pallas_call | solution.py:524
  48.8 2.7 %collective-permute-start.15 = (bf16[512,128]{1,0:T(8,128)(2,1)S(1)}, bf16[512,128]{1,0:T(8,128)(2,1)S(1)}, u32[]{:S(2)}, u32[]{:S(2)}) collective-permute-start(bf16[512,128]{1,0:T(8,128)(2,1)S(1)} %get-tuple-element.67), channel_id=1, source_target_pairs={{0,4},{1,5},{2,6},{3,7},{4,0},{5,1},{6,2},{7,3},{8,12},{9,13},{10,... | collective-permute-start | bytes 393224 | tf_op jit(solution)/shard_map/ppermute | solution.py:445
  52.6 7.3 %collective-permute-done.15.refs_1_.refs_2_ = bf16[512,128]{1,0:T(8,128)(2,1)S(1)} collective-permute-done((bf16[512,128]{1,0:T(8,128)(2,1)S(1)}, bf16[512,128]{1,0:T(8,128)(2,1)S(1)}, u32[]{:S(2)}, u32[]{:S(2)}) %collective-permute-start.15) | collective-permute-done | bytes 131104 | tf_op jit(solution)/shard_map/ppermute | solution.py:445
  59.9 2.0 %collective-permute-done.16.refs_2_.refs_3_ = bf16[512,128]{1,0:T(8,128)(2,1)S(1)} collective-permute-done((bf16[512,128]{1,0:T(8,128)(2,1)S(1)}, bf16[512,128]{1,0:T(8,128)(2,1)S(1)}, u32[]{:S(2)}, u32[]{:S(2)}) %collective-permute-start.16) | collective-permute-done | bytes 131104 | tf_op jit(solution)/shard_map/ppermute | solution.py:445
  63.5 3.7 %collective-permute-done.18.refs_1_ = bf16[1536,128]{1,0:T(8,128)(2,1)S(1)} collective-permute-done((bf16[1536,128]{1,0:T(8,128)(2,1)}, bf16[1536,128]{1,0:T(8,128)(2,1)S(1)}, u32[]{:S(2)}, u32[]{:S(2)}) %collective-permute-start.18) | collective-permute-done | bytes 393248 | tf_op jit(solution)/shard_map/ppermute | solution.py:445
  69.6 1.7 %collective-permute-start.23 = (bf16[512,128]{1,0:T(8,128)(2,1)S(1)}, bf16[512,128]{1,0:T(8,128)(2,1)S(1)}, u32[]{:S(2)}, u32[]{:S(2)}) collective-permute-start(bf16[512,128]{1,0:T(8,128)(2,1)S(1)} %get-tuple-element.81), channel_id=1, source_target_pairs={{0,5},{1,4},{2,7},{3,6},{4,1},{5,0},{6,3},{7,2},{8,13},{9,12},{10,... | collective-permute-start | bytes 393224 | tf_op jit(solution)/shard_map/ppermute | solution.py:445
  71.7 2.4 %collective-permute-done.20.refs_2_ = bf16[512,128]{1,0:T(8,128)(2,1)S(1)} collective-permute-done((bf16[512,128]{1,0:T(8,128)(2,1)S(1)}, bf16[512,128]{1,0:T(8,128)(2,1)S(1)}, u32[]{:S(2)}, u32[]{:S(2)}) %collective-permute-start.20) | collective-permute-done | bytes 131104 | tf_op jit(solution)/shard_map/ppermute | solution.py:445
  77.5 4.0 %collective-permute-done.24.refs_6_ = bf16[512,128]{1,0:T(8,128)(2,1)S(1)} collective-permute-done((bf16[512,128]{1,0:T(8,128)(2,1)S(1)}, bf16[512,128]{1,0:T(8,128)(2,1)S(1)}, u32[]{:S(2)}, u32[]{:S(2)}) %collective-permute-start.24) | collective-permute-done | bytes 131104 | tf_op jit(solution)/shard_map/ppermute | solution.py:445
  81.5 1.6 %collective-permute-done.25.refs_7_ = bf16[512,128]{1,0:T(8,128)(2,1)S(1)} collective-permute-done((bf16[512,128]{1,0:T(8,128)(2,1)S(1)}, bf16[512,128]{1,0:T(8,128)(2,1)S(1)}, u32[]{:S(2)}, u32[]{:S(2)}) %collective-permute-start.25) | collective-permute-done | bytes 131104 | tf_op jit(solution)/shard_map/ppermute | solution.py:445
  83.2 1.8 %gradient.1 = bf16[16,2,128,128]{3,2,1,0:T(8,128)(2,1)} custom-call(bf16[8,2,128,128]{3,2,1,0:T(8,128)(2,1)S(1)} %copy-done.1, s32[16]{0:T(128)S(4)} %get-tuple-element.71.freqs, bf16[512,128]{1,0:T(8,128)(2,1)S(1)} %get-tuple-element.76.refs_0_, bf16[512,128]{1,0:T(8,128)(2,1)S(1)} %collective-permute-done.19.refs_1_, ...), custom_call_target="tpu_custom_call" | custom-call | bytes 1048576 | tf_op jit(solution)/shard_map/gradient/pallas_call | solution.py:562
  (48 shorter events, 19.4 us)
Async XLA Ops:
  4.0 5.0 %collective-permute-start.2 = (bf16[528,128]{1,0:T(8,128)(2,1)S(1)}, bf16[528,128]{1,0:T(8,128)(2,1)S(1)}, u32[]{:S(2)}, u32[]{:S(2)}) collective-permute-start(bf16[528,128]{1,0:T(8,128)(2,1)S(1)} %get-tuple-element.48), channel_id=1, source_target_pairs={{0,1},{1,0},{2,3},{3,2},{4,5},{5,4},{6,7},{7,6},{8,9},{9,8},{10,11... | collective-permute-start | bytes 405512 | tf_op jit(solution)/shard_map/ppermute | solution.py:445
  4.5 7.1 %collective-permute-start.3 = (bf16[528,128]{1,0:T(8,128)(2,1)S(1)}, bf16[528,128]{1,0:T(8,128)(2,1)S(1)}, u32[]{:S(2)}, u32[]{:S(2)}) collective-permute-start(bf16[528,128]{1,0:T(8,128)(2,1)S(1)} %get-tuple-element.49), channel_id=1, source_target_pairs={{0,2},{1,3},{2,0},{3,1},{4,6},{5,7},{6,4},{7,5},{8,10},{9,11},{10,... | collective-permute-start | bytes 405512 | tf_op jit(solution)/shard_map/ppermute | solution.py:445
  7.1 6.8 %collective-permute-start.4 = (bf16[528,128]{1,0:T(8,128)(2,1)S(1)}, bf16[528,128]{1,0:T(8,128)(2,1)S(1)}, u32[]{:S(2)}, u32[]{:S(2)}) collective-permute-start(bf16[528,128]{1,0:T(8,128)(2,1)S(1)} %get-tuple-element.50), channel_id=1, source_target_pairs={{0,3},{1,2},{2,1},{3,0},{4,7},{5,6},{6,5},{7,4},{8,11},{9,10},{10,... | collective-permute-start | bytes 405512 | tf_op jit(solution)/shard_map/ppermute | solution.py:445
  7.1 6.7 %collective-permute-start.5 = (bf16[528,128]{1,0:T(8,128)(2,1)S(1)}, bf16[528,128]{1,0:T(8,128)(2,1)S(1)}, u32[]{:S(2)}, u32[]{:S(2)}) collective-permute-start(bf16[528,128]{1,0:T(8,128)(2,1)S(1)} %get-tuple-element.51), channel_id=1, source_target_pairs={{0,4},{1,5},{2,6},{3,7},{4,0},{5,1},{6,2},{7,3},{8,12},{9,13},{10,... | collective-permute-start | bytes 405512 | tf_op jit(solution)/shard_map/ppermute | solution.py:445
  8.9 6.8 %collective-permute-start.6 = (bf16[528,128]{1,0:T(8,128)(2,1)S(1)}, bf16[528,128]{1,0:T(8,128)(2,1)S(1)}, u32[]{:S(2)}, u32[]{:S(2)}) collective-permute-start(bf16[528,128]{1,0:T(8,128)(2,1)S(1)} %get-tuple-element.52), channel_id=1, source_target_pairs={{0,5},{1,4},{2,7},{3,6},{4,1},{5,0},{6,3},{7,2},{8,13},{9,12},{10,... | collective-permute-start | bytes 405512 | tf_op jit(solution)/shard_map/ppermute | solution.py:445
  8.9 11.5 %collective-permute-start.7 = (bf16[528,128]{1,0:T(8,128)(2,1)S(1)}, bf16[528,128]{1,0:T(8,128)(2,1)S(1)}, u32[]{:S(2)}, u32[]{:S(2)}) collective-permute-start(bf16[528,128]{1,0:T(8,128)(2,1)S(1)} %get-tuple-element.53), channel_id=1, source_target_pairs={{0,6},{1,7},{2,4},{3,5},{4,2},{5,3},{6,0},{7,1},{8,14},{9,15},{10,... | collective-permute-start | bytes 405512 | tf_op jit(solution)/shard_map/ppermute | solution.py:445
  11.6 10.7 %collective-permute-start.8 = (bf16[528,128]{1,0:T(8,128)(2,1)S(1)}, bf16[528,128]{1,0:T(8,128)(2,1)S(1)}, u32[]{:S(2)}, u32[]{:S(2)}) collective-permute-start(bf16[528,128]{1,0:T(8,128)(2,1)S(1)} %get-tuple-element.54), channel_id=1, source_target_pairs={{0,7},{1,6},{2,5},{3,4},{4,3},{5,2},{6,1},{7,0},{8,15},{9,14},{10,... | collective-permute-start | bytes 405512 | tf_op jit(solution)/shard_map/ppermute | solution.py:445
  23.3 21.0 %collective-permute-start.13 = (bf16[1552,128]{1,0:T(8,128)(2,1)S(1)}, bf16[1552,128]{1,0:T(8,128)(2,1)S(1)}, u32[]{:S(2)}, u32[]{:S(2)}) collective-permute-start(bf16[1552,128]{1,0:T(8,128)(2,1)S(1)} %get-tuple-element.63.mine), channel_id=1, source_target_pairs={{0,8},{1,9},{2,10},{3,11},{4,12},{5,13},{6,14},{7,15},{8,0},{9,1},... | collective-permute-start | bytes 1191944 | tf_op jit(solution)/shard_map/ppermute | solution.py:445
  26.7 5.5 %collective-permute-start.9 = (bf16[512,128]{1,0:T(8,128)(2,1)S(1)}, bf16[512,128]{1,0:T(8,128)(2,1)S(1)}, u32[]{:S(2)}, u32[]{:S(2)}) collective-permute-start(bf16[512,128]{1,0:T(8,128)(2,1)S(1)} %get-tuple-element.59), channel_id=1, source_target_pairs={{0,2},{1,3},{2,0},{3,1},{4,6},{5,7},{6,4},{7,5},{8,10},{9,11},{10,... | collective-permute-start | bytes 393224 | tf_op jit(solution)/shard_map/ppermute | solution.py:445
  27.3 11.1 %collective-permute-start.10 = (bf16[512,128]{1,0:T(8,128)(2,1)S(1)}, bf16[512,128]{1,0:T(8,128)(2,1)S(1)}, u32[]{:S(2)}, u32[]{:S(2)}) collective-permute-start(bf16[512,128]{1,0:T(8,128)(2,1)S(1)} %get-tuple-element.60), channel_id=1, source_target_pairs={{0,4},{1,5},{2,6},{3,7},{4,0},{5,1},{6,2},{7,3},{8,12},{9,13},{10,... | collective-permute-start | bytes 393224 | tf_op jit(solution)/shard_map/ppermute | solution.py:445
  28.8 11.8 %collective-permute-start.11 = (bf16[512,128]{1,0:T(8,128)(2,1)S(1)}, bf16[512,128]{1,0:T(8,128)(2,1)S(1)}, u32[]{:S(2)}, u32[]{:S(2)}) collective-permute-start(bf16[512,128]{1,0:T(8,128)(2,1)S(1)} %get-tuple-element.61), channel_id=1, source_target_pairs={{0,6},{1,7},{2,4},{3,5},{4,2},{5,3},{6,0},{7,1},{8,14},{9,15},{10,... | collective-permute-start | bytes 393224 | tf_op jit(solution)/shard_map/ppermute | solution.py:445
  40.7 1.6 %collective-permute-start.12 = (bf16[1024,128]{1,0:T(8,128)(2,1)S(1)}, bf16[1024,128]{1,0:T(8,128)(2,1)S(1)}, u32[]{:S(2)}, u32[]{:S(2)}) collective-permute-start(bf16[1024,128]{1,0:T(8,128)(2,1)S(1)} %for_mate.2), channel_id=1, source_target_pairs={{0,1},{1,0},{2,3},{3,2},{4,5},{5,4},{6,7},{7,6},{8,9},{9,8},{10,11... | collective-permute-start | bytes 786440 | tf_op jit(solution)/shard_map/ppermute | solution.py:445
  47.0 20.2 %collective-permute-start.18 = (bf16[1536,128]{1,0:T(8,128)(2,1)}, bf16[1536,128]{1,0:T(8,128)(2,1)S(1)}, u32[]{:S(2)}, u32[]{:S(2)}) collective-permute-start(bf16[1536,128]{1,0:T(8,128)(2,1)} %get-tuple-element.74), channel_id=1, source_target_pairs={{0,8},{1,9},{2,10},{3,11},{4,12},{5,13},{6,14},{7,15},{8,0},{9,1},... | collective-permute-start | bytes 1179656 | tf_op jit(solution)/shard_map/ppermute | solution.py:445
  47.3 5.3 %collective-permute-start.14 = (bf16[512,128]{1,0:T(8,128)(2,1)S(1)}, bf16[512,128]{1,0:T(8,128)(2,1)S(1)}, u32[]{:S(2)}, u32[]{:S(2)}) collective-permute-start(bf16[512,128]{1,0:T(8,128)(2,1)S(1)} %get-tuple-element.66), channel_id=1, source_target_pairs={{0,2},{1,3},{2,0},{3,1},{4,6},{5,7},{6,4},{7,5},{8,10},{9,11},{10,... | collective-permute-start | bytes 393224 | tf_op jit(solution)/shard_map/ppermute | solution.py:445
  48.8 11.0 %collective-permute-start.15 = (bf16[512,128]{1,0:T(8,128)(2,1)S(1)}, bf16[512,128]{1,0:T(8,128)(2,1)S(1)}, u32[]{:S(2)}, u32[]{:S(2)}) collective-permute-start(bf16[512,128]{1,0:T(8,128)(2,1)S(1)} %get-tuple-element.67), channel_id=1, source_target_pairs={{0,4},{1,5},{2,6},{3,7},{4,0},{5,1},{6,2},{7,3},{8,12},{9,13},{10,... | collective-permute-start | bytes 393224 | tf_op jit(solution)/shard_map/ppermute | solution.py:445
  51.6 10.3 %collective-permute-start.16 = (bf16[512,128]{1,0:T(8,128)(2,1)S(1)}, bf16[512,128]{1,0:T(8,128)(2,1)S(1)}, u32[]{:S(2)}, u32[]{:S(2)}) collective-permute-start(bf16[512,128]{1,0:T(8,128)(2,1)S(1)} %get-tuple-element.68), channel_id=1, source_target_pairs={{0,6},{1,7},{2,4},{3,5},{4,2},{5,3},{6,0},{7,1},{8,14},{9,15},{10,... | collective-permute-start | bytes 393224 | tf_op jit(solution)/shard_map/ppermute | solution.py:445
  61.9 7.6 %collective-permute-start.17 = (bf16[1024,128]{1,0:T(8,128)(2,1)S(1)}, bf16[1024,128]{1,0:T(8,128)(2,1)S(1)}, u32[]{:S(2)}, u32[]{:S(2)}) collective-permute-start(bf16[1024,128]{1,0:T(8,128)(2,1)S(1)} %for_mate.3), channel_id=1, source_target_pairs={{0,1},{1,0},{2,3},{3,2},{4,5},{5,4},{6,7},{7,6},{8,9},{9,8},{10,11... | collective-permute-start | bytes 786440 | tf_op jit(solution)/shard_map/ppermute | solution.py:445
  67.6 3.6 %collective-permute-start.19 = (bf16[512,128]{1,0:T(8,128)(2,1)S(1)}, bf16[512,128]{1,0:T(8,128)(2,1)S(1)}, u32[]{:S(2)}, u32[]{:S(2)}) collective-permute-start(bf16[512,128]{1,0:T(8,128)(2,1)S(1)} %get-tuple-element.77), channel_id=1, source_target_pairs={{0,1},{1,0},{2,3},{3,2},{4,5},{5,4},{6,7},{7,6},{8,9},{9,8},{10,11... | collective-permute-start | bytes 393224 | tf_op jit(solution)/shard_map/ppermute | solution.py:445
  67.7 6.4 %collective-permute-start.20 = (bf16[512,128]{1,0:T(8,128)(2,1)S(1)}, bf16[512,128]{1,0:T(8,128)(2,1)S(1)}, u32[]{:S(2)}, u32[]{:S(2)}) collective-permute-start(bf16[512,128]{1,0:T(8,128)(2,1)S(1)} %get-tuple-element.78), channel_id=1, source_target_pairs={{0,2},{1,3},{2,0},{3,1},{4,6},{5,7},{6,4},{7,5},{8,10},{9,11},{10,... | collective-permute-start | bytes 393224 | tf_op jit(solution)/shard_map/ppermute | solution.py:445
  68.3 7.6 %collective-permute-start.21 = (bf16[512,128]{1,0:T(8,128)(2,1)S(1)}, bf16[512,128]{1,0:T(8,128)(2,1)S(1)}, u32[]{:S(2)}, u32[]{:S(2)}) collective-permute-start(bf16[512,128]{1,0:T(8,128)(2,1)S(1)} %get-tuple-element.79), channel_id=1, source_target_pairs={{0,3},{1,2},{2,1},{3,0},{4,7},{5,6},{6,5},{7,4},{8,11},{9,10},{10,... | collective-permute-start | bytes 393224 | tf_op jit(solution)/shard_map/ppermute | solution.py:445
  69.6 6.4 %collective-permute-start.22 = (bf16[512,128]{1,0:T(8,128)(2,1)S(1)}, bf16[512,128]{1,0:T(8,128)(2,1)S(1)}, u32[]{:S(2)}, u32[]{:S(2)}) collective-permute-start(bf16[512,128]{1,0:T(8,128)(2,1)S(1)} %get-tuple-element.80), channel_id=1, source_target_pairs={{0,4},{1,5},{2,6},{3,7},{4,0},{5,1},{6,2},{7,3},{8,12},{9,13},{10,... | collective-permute-start | bytes 393224 | tf_op jit(solution)/shard_map/ppermute | solution.py:445
  69.6 8.0 %collective-permute-start.23 = (bf16[512,128]{1,0:T(8,128)(2,1)S(1)}, bf16[512,128]{1,0:T(8,128)(2,1)S(1)}, u32[]{:S(2)}, u32[]{:S(2)}) collective-permute-start(bf16[512,128]{1,0:T(8,128)(2,1)S(1)} %get-tuple-element.81), channel_id=1, source_target_pairs={{0,5},{1,4},{2,7},{3,6},{4,1},{5,0},{6,3},{7,2},{8,13},{9,12},{10,... | collective-permute-start | bytes 393224 | tf_op jit(solution)/shard_map/ppermute | solution.py:445
  71.3 10.3 %collective-permute-start.24 = (bf16[512,128]{1,0:T(8,128)(2,1)S(1)}, bf16[512,128]{1,0:T(8,128)(2,1)S(1)}, u32[]{:S(2)}, u32[]{:S(2)}) collective-permute-start(bf16[512,128]{1,0:T(8,128)(2,1)S(1)} %get-tuple-element.82), channel_id=1, source_target_pairs={{0,6},{1,7},{2,4},{3,5},{4,2},{5,3},{6,0},{7,1},{8,14},{9,15},{10,... | collective-permute-start | bytes 393224 | tf_op jit(solution)/shard_map/ppermute | solution.py:445
  74.1 9.1 %collective-permute-start.25 = (bf16[512,128]{1,0:T(8,128)(2,1)S(1)}, bf16[512,128]{1,0:T(8,128)(2,1)S(1)}, u32[]{:S(2)}, u32[]{:S(2)}) collective-permute-start(bf16[512,128]{1,0:T(8,128)(2,1)S(1)} %get-tuple-element.83), channel_id=1, source_target_pairs={{0,7},{1,6},{2,5},{3,4},{4,3},{5,2},{6,1},{7,0},{8,15},{9,14},{10,... | collective-permute-start | bytes 393224 | tf_op jit(solution)/shard_map/ppermute | solution.py:445
  (5 other events, 21.8 us)

commit v3 on v2

--- a/solution.py
+++ b/solution.py
@@ -18,7 +18,7 @@
 ANY = pl.BlockSpec(memory_space=pl.ANY)
 
 
-def call(kernel, name, out_shape, in_specs, scratch=(), out_specs=None, mib=24):
+def call(kernel, name, out_shape, in_specs, scratch=(), out_specs=None, mib=24, aliases=None):
     return pl.pallas_call(
         kernel,
         name=name,
@@ -26,6 +26,7 @@
         in_specs=in_specs,
         out_specs=out_specs or jax.tree.map(lambda _: VMEM, out_shape),
         scratch_shapes=list(scratch),
+        input_output_aliases=aliases or {},
         cost_estimate=pl.CostEstimate(flops=0, bytes_accessed=1 << 20, transcendentals=0),
         compiler_params=pltpu.CompilerParams(vmem_limit_bytes=mib * 1024 * 1024),
     )
@@ -381,26 +382,27 @@
             residual[f, 1, at, :] = imag[at] - wide[rows, :]
 
 
-def gradient_kernel(source, freqs, *refs):
-    parts, (gradient_hbm, gradient, wide, sems) = refs[:GROUP], refs[GROUP:]
-    slots, _, block, _ = gradient.shape
+def gradient_kernel(members, source, freqs, *refs):
+    parts, (gradient_hbm, gradient, wide, sems) = refs[: len(members)], refs[-4:]
+    slots, _, _, block = gradient.shape
     size, shots = parts[0].shape
     height = size // slots
     piece = height // 2
     scale = 1.0 / shots
-    for k in range(GROUP):
-        wide[member_rows(k, size)] = parts[k][...].astype(F32)
+    local = local_index()
+    for i, part in enumerate(parts):
+        wide[i * size : (i + 1) * size] = part[...].astype(F32)
 
     def one(t, carry):
-        left = wide[pl.ds(t, GROUP * height, stride=slots), :].astype(BF16)
+        left = wide[pl.ds(t, len(members) * height, stride=slots), :].astype(BF16)
         right = source[freqs[t]].reshape(2 * block, shots)
         total = -scale * lax.dot_general(
             left, right, (((1,), (1,)), ((), ())), preferred_element_type=F32
         )
         real, imag = [], []
-        for j in range(GROUP):
-            upper = total[j * height : j * height + piece]
-            lower = total[j * height + piece : (j + 1) * height]
+        for i in range(len(members)):
+            upper = total[i * height : i * height + piece]
+            lower = total[i * height + piece : (i + 1) * height]
             real.append(upper[:, :block] + lower[:, block:])
             imag.append(lower[:, :block] - upper[:, block:])
         gradient[t, 0] = jnp.concatenate(real, axis=0).astype(BF16)
@@ -410,13 +412,19 @@
     copies = []
     quarters = 4
     step = slots // quarters
-    for i in range(quarters):
-        lax.fori_loop(i * step, (i + 1) * step, one, 0, unroll=4)
-        at = pl.ds(i * step, step)
-        copies.append(
-            pltpu.make_async_copy(gradient.at[at], gradient_hbm.at[at], sems.at[i])
-        )
-        copies[-1].start()
+    for quarter in range(quarters):
+        lax.fori_loop(quarter * step, (quarter + 1) * step, one, 0, unroll=4)
+        at = pl.ds(quarter * step, step)
+        for i, k in enumerate(members):
+            rows = pl.ds(pl.multiple_of((local ^ k) * piece, piece), piece)
+            copies.append(
+                pltpu.make_async_copy(
+                    gradient.at[at, :, pl.ds(i * piece, piece), :],
+                    gradient_hbm.at[at, :, rows, :],
+                    sems.at[quarter * len(members) + i],
+                )
+            )
+            copies[-1].start()
     for copy in copies:
         copy.wait()
 
@@ -559,18 +567,26 @@
         [VMEM] * 2 + ([SMEM, VMEM, ANY] if groups == 2 else [VMEM] * len(got)),
         scratch=rest_rows + [pltpu.SemaphoreType.DMA] * len(rests),
     )(hot, rounded, *got)
-    gradient = call(
-        gradient_kernel,
-        "gradient",
-        jax.ShapeDtypeStruct(tiles.shape, BF16),
-        [VMEM, SMEM] + [VMEM] * GROUP,
-        out_specs=HBM,
-        scratch=[
-            pltpu.VMEM(tiles.shape, BF16),
-            wide,
-            pltpu.SemaphoreType.DMA((4,)),
-        ],
-    )(source, freqs, *in_group(out))
+    got = in_group(out)
+    gradient = []
+    for members in (range(GROUP - 2), range(GROUP - 2, GROUP)):
+        rows = len(members) * block // GROUP
+        gradient = [
+            call(
+                functools.partial(gradient_kernel, members),
+                "gradient",
+                in_hbm(tiles),
+                [VMEM, SMEM] + [VMEM] * len(members) + [ANY] * len(gradient),
+                out_specs=HBM,
+                scratch=[
+                    pltpu.VMEM((slots, 2, rows, block), BF16),
+                    pltpu.VMEM(((len(members) * height + 1) * slots, shots), F32),
+                    pltpu.SemaphoreType.DMA((4 * len(members),)),
+                ],
+                aliases={2 + len(members): 0} if gradient else None,
+            )(source, freqs, *[got[k] for k in members], *gradient)
+        ]
+    gradient = gradient[0]
     return residual, gradient
 
 

time: 85.2 us -> 84.6 us (level)
  waiting for transfers between devices: 46.1 us -> 44.4 us
  Pallas kernels: 9.91 us -> 11 us
    ppermute x24, waiting for transfers between devices: 46.1 us -> 44.4 us  [swap(): lax.ppermute(value, 'tiles', [(i, i ^ distance) for i in range(peers)])]
    pallas_call x1 -> x2, Pallas kernels: 1.76 us -> 2.87 us  [per_device(): call(functools.partial(gradient_kernel, members), 'gradient', in_hbm(tile...]
  transfers between devices with their start and end apart: 24 -> 24, of which waited for: 18 -> 18; matrix products, arithmetic and copies ran while one was open for 1% -> 1% of each run, Pallas kernels for 3% -> 5%
where the time goes in v3:
time: 84.6 us; the launch traced here: 84.3 us
  waiting for transfers between devices  44.4 us (52%)
  starting transfers between devices  25.3 us (30%)
  Pallas kernels  11 us (13%)
  local copies, waits for them, and re-layouts  2.15 us (3%)
  between operations  1.41 us (2%)
    ppermute x24, waiting for transfers between devices, swap(): lax.ppermute(value, 'tiles', [(i, i ^ distance) for i in range(peers)])  44.4 us
    ppermute x24, starting transfers between devices, swap(): lax.ppermute(value, 'tiles', [(i, i ^ distance) for i in range(peers)])  25.3 us
    pallas_call x2, Pallas kernels, per_device(): call(functools.partial(gradient_kernel, members), 'gradient', in_hbm(tile...  2.87 us
    pallas_call x1, Pallas kernels, per_device(): call(parts_kernel, 'parts', [in_hbm(shape(freq_count, 2, block)), in_hbm(...  2.67 us
    pallas_call x1, Pallas kernels, per_device(): call(functools.partial(residual_kernel, sizes), 'residual_slices', [shape...  1.86 us
  transfers between devices with their start and end apart: 24, of which 18 were waited for; matrix products, arithmetic and copies ran while one was open for 1% of the time, Pallas kernels for 5%

profile of v3, /device:TPU:0, one launch (start us, length us, event | category | flops | bytes accessed | tf_op | source)
XLA Modules:
  0.0 84.3 jit_solution(7377877369890933371)
XLA Ops:
  1.3 2.7 %parts.1 = (bf16[8,2,128,128]{3,2,1,0:T(8,128)(2,1)}, bf16[256,128]{1,0:T(8,128)(2,1)}, s32[16]{0:T(128)S(4)}, bf16[528,128]{1,0:T(8,128)(2,1)S(1)}, bf16[528,12...) custom-call(bf16[8,2,128,128]{3,2,1,0:T(8,128)(2,1)} %data.3, ...), custom_call_target="tpu_custom_call" | custom-call | bytes 1048576 | tf_op jit(solution)/shard_map/parts/pallas_call | solution.py:469
  4.5 2.6 %collective-permute-start.3 = (bf16[528,128]{1,0:T(8,128)(2,1)S(1)}, bf16[528,128]{1,0:T(8,128)(2,1)S(1)}, u32[]{:S(2)}, u32[]{:S(2)}) collective-permute-start(bf16[528,128]{1,0:T(8,128)(2,1)S(1)} %get-tuple-element.49), channel_id=1, source_target_pairs={{0,2},{1,3},{2,0},{3,1},{4,6},{5,7},{6,4},{7,5},{8,10},{9,11},{10,... | collective-permute-start | bytes 405512 | tf_op jit(solution)/shard_map/ppermute | solution.py:453
  7.1 1.8 %collective-permute-start.5 = (bf16[528,128]{1,0:T(8,128)(2,1)S(1)}, bf16[528,128]{1,0:T(8,128)(2,1)S(1)}, u32[]{:S(2)}, u32[]{:S(2)}) collective-permute-start(bf16[528,128]{1,0:T(8,128)(2,1)S(1)} %get-tuple-element.51), channel_id=1, source_target_pairs={{0,4},{1,5},{2,6},{3,7},{4,0},{5,1},{6,2},{7,3},{8,12},{9,13},{10,... | collective-permute-start | bytes 405512 | tf_op jit(solution)/shard_map/ppermute | solution.py:453
  8.9 2.6 %collective-permute-start.7 = (bf16[528,128]{1,0:T(8,128)(2,1)S(1)}, bf16[528,128]{1,0:T(8,128)(2,1)S(1)}, u32[]{:S(2)}, u32[]{:S(2)}) collective-permute-start(bf16[528,128]{1,0:T(8,128)(2,1)S(1)} %get-tuple-element.53), channel_id=1, source_target_pairs={{0,6},{1,7},{2,4},{3,5},{4,2},{5,3},{6,0},{7,1},{8,14},{9,15},{10,... | collective-permute-start | bytes 405512 | tf_op jit(solution)/shard_map/ppermute | solution.py:453
  11.6 1.7 %collective-permute-start.8 = (bf16[528,128]{1,0:T(8,128)(2,1)S(1)}, bf16[528,128]{1,0:T(8,128)(2,1)S(1)}, u32[]{:S(2)}, u32[]{:S(2)}) collective-permute-start(bf16[528,128]{1,0:T(8,128)(2,1)S(1)} %get-tuple-element.54), channel_id=1, source_target_pairs={{0,7},{1,6},{2,5},{3,4},{4,3},{5,2},{6,1},{7,0},{8,15},{9,14},{10,... | collective-permute-start | bytes 405512 | tf_op jit(solution)/shard_map/ppermute | solution.py:453
  13.9 1.9 %collective-permute-done.6.refs_5_ = bf16[528,128]{1,0:T(8,128)(2,1)S(1)} collective-permute-done((bf16[528,128]{1,0:T(8,128)(2,1)S(1)}, bf16[528,128]{1,0:T(8,128)(2,1)S(1)}, u32[]{:S(2)}, u32[]{:S(2)}) %collective-permute-start.6) | collective-permute-done | bytes 135200 | tf_op jit(solution)/shard_map/ppermute | solution.py:453
  15.8 4.7 %collective-permute-done.7.refs_6_ = bf16[528,128]{1,0:T(8,128)(2,1)S(1)} collective-permute-done((bf16[528,128]{1,0:T(8,128)(2,1)S(1)}, bf16[528,128]{1,0:T(8,128)(2,1)S(1)}, u32[]{:S(2)}, u32[]{:S(2)}) %collective-permute-start.7) | collective-permute-done | bytes 135200 | tf_op jit(solution)/shard_map/ppermute | solution.py:453
  20.5 1.8 %collective-permute-done.8.refs_7_ = bf16[528,128]{1,0:T(8,128)(2,1)S(1)} collective-permute-done((bf16[528,128]{1,0:T(8,128)(2,1)S(1)}, bf16[528,128]{1,0:T(8,128)(2,1)S(1)}, u32[]{:S(2)}, u32[]{:S(2)}) %collective-permute-start.8) | collective-permute-done | bytes 135200 | tf_op jit(solution)/shard_map/ppermute | solution.py:453
  23.3 2.7 %collective-permute-start.13 = (bf16[1552,128]{1,0:T(8,128)(2,1)S(1)}, bf16[1552,128]{1,0:T(8,128)(2,1)S(1)}, u32[]{:S(2)}, u32[]{:S(2)}) collective-permute-start(bf16[1552,128]{1,0:T(8,128)(2,1)S(1)} %get-tuple-element.63.mine), channel_id=1, source_target_pairs={{0,8},{1,9},{2,10},{3,11},{4,12},{5,13},{6,14},{7,15},{8,0},{9,1},... | collective-permute-start | bytes 1191944 | tf_op jit(solution)/shard_map/ppermute | solution.py:453
  27.3 1.6 %collective-permute-start.10 = (bf16[512,128]{1,0:T(8,128)(2,1)S(1)}, bf16[512,128]{1,0:T(8,128)(2,1)S(1)}, u32[]{:S(2)}, u32[]{:S(2)}) collective-permute-start(bf16[512,128]{1,0:T(8,128)(2,1)S(1)} %get-tuple-element.60), channel_id=1, source_target_pairs={{0,4},{1,5},{2,6},{3,7},{4,0},{5,1},{6,2},{7,3},{8,12},{9,13},{10,... | collective-permute-start | bytes 393224 | tf_op jit(solution)/shard_map/ppermute | solution.py:453
  30.2 2.0 %collective-permute-done.9.refs_0_.refs_1_ = bf16[512,128]{1,0:T(8,128)(2,1)S(1)} collective-permute-done((bf16[512,128]{1,0:T(8,128)(2,1)S(1)}, bf16[512,128]{1,0:T(8,128)(2,1)S(1)}, u32[]{:S(2)}, u32[]{:S(2)}) %collective-permute-start.9) | collective-permute-done | bytes 131104 | tf_op jit(solution)/shard_map/ppermute | solution.py:453
  32.2 6.1 %collective-permute-done.10.refs_1_.refs_2_ = bf16[512,128]{1,0:T(8,128)(2,1)S(1)} collective-permute-done((bf16[512,128]{1,0:T(8,128)(2,1)S(1)}, bf16[512,128]{1,0:T(8,128)(2,1)S(1)}, u32[]{:S(2)}, u32[]{:S(2)}) %collective-permute-start.10) | collective-permute-done | bytes 131104 | tf_op jit(solution)/shard_map/ppermute | solution.py:453
  38.4 2.3 %collective-permute-done.11.refs_2_.refs_3_ = bf16[512,128]{1,0:T(8,128)(2,1)S(1)} collective-permute-done((bf16[512,128]{1,0:T(8,128)(2,1)S(1)}, bf16[512,128]{1,0:T(8,128)(2,1)S(1)}, u32[]{:S(2)}, u32[]{:S(2)}) %collective-permute-start.11) | collective-permute-done | bytes 131104 | tf_op jit(solution)/shard_map/ppermute | solution.py:453
  42.3 2.0 %collective-permute-done.13.got.refs_6_ = bf16[1552,128]{1,0:T(8,128)(2,1)S(1)} collective-permute-done((bf16[1552,128]{1,0:T(8,128)(2,1)S(1)}, bf16[1552,128]{1,0:T(8,128)(2,1)S(1)}, u32[]{:S(2)}, u32[]{:S(2)}) %collective-permute-start.13) | collective-permute-done | bytes 397344 | tf_op jit(solution)/shard_map/ppermute | solution.py:453
  45.1 1.9 %residual_slices.1 = (bf16[32,64,128]{2,1,0:T(8,128)(2,1)S(1)}, bf16[1536,128]{1,0:T(8,128)(2,1)}, bf16[32,16,128]{2,1,0:T(8,128)(2,1)}, bf16[256,128]{1,0:T(8,1...) custom-call(f32[32,64,128]{2,1,0:T(8,128)S(1)} %get-tuple-element.55, ...), custom_call_target="tpu_custom_call" | custom-call | bytes 1048576 | tf_op jit(solution)/shard_map/residual_slices/pallas_call | solution.py:532
  48.8 2.7 %collective-permute-start.15 = (bf16[512,128]{1,0:T(8,128)(2,1)S(1)}, bf16[512,128]{1,0:T(8,128)(2,1)S(1)}, u32[]{:S(2)}, u32[]{:S(2)}) collective-permute-start(bf16[512,128]{1,0:T(8,128)(2,1)S(1)} %get-tuple-element.67), channel_id=1, source_target_pairs={{0,4},{1,5},{2,6},{3,7},{4,0},{5,1},{6,2},{7,3},{8,12},{9,13},{10,... | collective-permute-start | bytes 393224 | tf_op jit(solution)/shard_map/ppermute | solution.py:453
  52.6 7.3 %collective-permute-done.15.refs_1_.refs_2_ = bf16[512,128]{1,0:T(8,128)(2,1)S(1)} collective-permute-done((bf16[512,128]{1,0:T(8,128)(2,1)S(1)}, bf16[512,128]{1,0:T(8,128)(2,1)S(1)}, u32[]{:S(2)}, u32[]{:S(2)}) %collective-permute-start.15) | collective-permute-done | bytes 131104 | tf_op jit(solution)/shard_map/ppermute | solution.py:453
  59.9 2.0 %collective-permute-done.16.refs_2_.refs_3_ = bf16[512,128]{1,0:T(8,128)(2,1)S(1)} collective-permute-done((bf16[512,128]{1,0:T(8,128)(2,1)S(1)}, bf16[512,128]{1,0:T(8,128)(2,1)S(1)}, u32[]{:S(2)}, u32[]{:S(2)}) %collective-permute-start.16) | collective-permute-done | bytes 131104 | tf_op jit(solution)/shard_map/ppermute | solution.py:453
  63.5 3.7 %collective-permute-done.18.refs_1_ = bf16[1536,128]{1,0:T(8,128)(2,1)S(1)} collective-permute-done((bf16[1536,128]{1,0:T(8,128)(2,1)}, bf16[1536,128]{1,0:T(8,128)(2,1)S(1)}, u32[]{:S(2)}, u32[]{:S(2)}) %collective-permute-start.18) | collective-permute-done | bytes 393248 | tf_op jit(solution)/shard_map/ppermute | solution.py:453
  69.6 1.7 %collective-permute-start.25 = (bf16[512,128]{1,0:T(8,128)(2,1)S(1)}, bf16[512,128]{1,0:T(8,128)(2,1)S(1)}, u32[]{:S(2)}, u32[]{:S(2)}) collective-permute-start(bf16[512,128]{1,0:T(8,128)(2,1)S(1)} %get-tuple-element.83), channel_id=1, source_target_pairs={{0,5},{1,4},{2,7},{3,6},{4,1},{5,0},{6,3},{7,2},{8,13},{9,12},{10,... | collective-permute-start | bytes 393224 | tf_op jit(solution)/shard_map/ppermute | solution.py:453
  71.7 2.4 %collective-permute-done.22.refs_2_ = bf16[512,128]{1,0:T(8,128)(2,1)S(1)} collective-permute-done((bf16[512,128]{1,0:T(8,128)(2,1)S(1)}, bf16[512,128]{1,0:T(8,128)(2,1)S(1)}, u32[]{:S(2)}, u32[]{:S(2)}) %collective-permute-start.22) | collective-permute-done | bytes 131104 | tf_op jit(solution)/shard_map/ppermute | solution.py:453
  77.5 1.7 %gradient.2.refs_2_ = bf16[16,2,128,128]{3,2,1,0:T(8,128)(2,1)} custom-call(bf16[8,2,128,128]{3,2,1,0:T(8,128)(2,1)S(1)} %copy-done.1, s32[16]{0:T(128)S(4)} %get-tuple-element.71.freqs, bf16[512,128]{1,0:T(8,128)(2,1)S(1)} %get-tuple-element.78.refs_0_, bf16[512,128]{1,0:T(8,128)(2,1)S(1)} %collective-permute-done.21.refs_1_, ...), custom_call_target="tpu_custom_call" | custom-call | bytes 1048576 | tf_op jit(solution)/shard_map/gradient/pallas_call | solution.py:575
  79.2 2.3 %collective-permute-done.19.refs_0_ = bf16[512,128]{1,0:T(8,128)(2,1)S(1)} collective-permute-done((bf16[512,128]{1,0:T(8,128)(2,1)S(1)}, bf16[512,128]{1,0:T(8,128)(2,1)S(1)}, u32[]{:S(2)}, u32[]{:S(2)}) %collective-permute-start.19) | collective-permute-done | bytes 131104 | tf_op jit(solution)/shard_map/ppermute | solution.py:453
  81.5 1.6 %collective-permute-done.20.refs_1_ = bf16[512,128]{1,0:T(8,128)(2,1)S(1)} collective-permute-done((bf16[512,128]{1,0:T(8,128)(2,1)S(1)}, bf16[512,128]{1,0:T(8,128)(2,1)S(1)}, u32[]{:S(2)}, u32[]{:S(2)}) %collective-permute-start.20) | collective-permute-done | bytes 131104 | tf_op jit(solution)/shard_map/ppermute | solution.py:453
  (49 shorter events, 20.6 us)
Async XLA Ops:
  4.0 5.0 %collective-permute-start.2 = (bf16[528,128]{1,0:T(8,128)(2,1)S(1)}, bf16[528,128]{1,0:T(8,128)(2,1)S(1)}, u32[]{:S(2)}, u32[]{:S(2)}) collective-permute-start(bf16[528,128]{1,0:T(8,128)(2,1)S(1)} %get-tuple-element.48), channel_id=1, source_target_pairs={{0,1},{1,0},{2,3},{3,2},{4,5},{5,4},{6,7},{7,6},{8,9},{9,8},{10,11... | collective-permute-start | bytes 405512 | tf_op jit(solution)/shard_map/ppermute | solution.py:453
  4.5 7.1 %collective-permute-start.3 = (bf16[528,128]{1,0:T(8,128)(2,1)S(1)}, bf16[528,128]{1,0:T(8,128)(2,1)S(1)}, u32[]{:S(2)}, u32[]{:S(2)}) collective-permute-start(bf16[528,128]{1,0:T(8,128)(2,1)S(1)} %get-tuple-element.49), channel_id=1, source_target_pairs={{0,2},{1,3},{2,0},{3,1},{4,6},{5,7},{6,4},{7,5},{8,10},{9,11},{10,... | collective-permute-start | bytes 405512 | tf_op jit(solution)/shard_map/ppermute | solution.py:453
  7.1 6.8 %collective-permute-start.4 = (bf16[528,128]{1,0:T(8,128)(2,1)S(1)}, bf16[528,128]{1,0:T(8,128)(2,1)S(1)}, u32[]{:S(2)}, u32[]{:S(2)}) collective-permute-start(bf16[528,128]{1,0:T(8,128)(2,1)S(1)} %get-tuple-element.50), channel_id=1, source_target_pairs={{0,3},{1,2},{2,1},{3,0},{4,7},{5,6},{6,5},{7,4},{8,11},{9,10},{10,... | collective-permute-start | bytes 405512 | tf_op jit(solution)/shard_map/ppermute | solution.py:453
  7.1 6.7 %collective-permute-start.5 = (bf16[528,128]{1,0:T(8,128)(2,1)S(1)}, bf16[528,128]{1,0:T(8,128)(2,1)S(1)}, u32[]{:S(2)}, u32[]{:S(2)}) collective-permute-start(bf16[528,128]{1,0:T(8,128)(2,1)S(1)} %get-tuple-element.51), channel_id=1, source_target_pairs={{0,4},{1,5},{2,6},{3,7},{4,0},{5,1},{6,2},{7,3},{8,12},{9,13},{10,... | collective-permute-start | bytes 405512 | tf_op jit(solution)/shard_map/ppermute | solution.py:453
  8.9 6.8 %collective-permute-start.6 = (bf16[528,128]{1,0:T(8,128)(2,1)S(1)}, bf16[528,128]{1,0:T(8,128)(2,1)S(1)}, u32[]{:S(2)}, u32[]{:S(2)}) collective-permute-start(bf16[528,128]{1,0:T(8,128)(2,1)S(1)} %get-tuple-element.52), channel_id=1, source_target_pairs={{0,5},{1,4},{2,7},{3,6},{4,1},{5,0},{6,3},{7,2},{8,13},{9,12},{10,... | collective-permute-start | bytes 405512 | tf_op jit(solution)/shard_map/ppermute | solution.py:453
  8.9 11.5 %collective-permute-start.7 = (bf16[528,128]{1,0:T(8,128)(2,1)S(1)}, bf16[528,128]{1,0:T(8,128)(2,1)S(1)}, u32[]{:S(2)}, u32[]{:S(2)}) collective-permute-start(bf16[528,128]{1,0:T(8,128)(2,1)S(1)} %get-tuple-element.53), channel_id=1, source_target_pairs={{0,6},{1,7},{2,4},{3,5},{4,2},{5,3},{6,0},{7,1},{8,14},{9,15},{10,... | collective-permute-start | bytes 405512 | tf_op jit(solution)/shard_map/ppermute | solution.py:453
  11.6 10.7 %collective-permute-start.8 = (bf16[528,128]{1,0:T(8,128)(2,1)S(1)}, bf16[528,128]{1,0:T(8,128)(2,1)S(1)}, u32[]{:S(2)}, u32[]{:S(2)}) collective-permute-start(bf16[528,128]{1,0:T(8,128)(2,1)S(1)} %get-tuple-element.54), channel_id=1, source_target_pairs={{0,7},{1,6},{2,5},{3,4},{4,3},{5,2},{6,1},{7,0},{8,15},{9,14},{10,... | collective-permute-start | bytes 405512 | tf_op jit(solution)/shard_map/ppermute | solution.py:453
  23.3 21.0 %collective-permute-start.13 = (bf16[1552,128]{1,0:T(8,128)(2,1)S(1)}, bf16[1552,128]{1,0:T(8,128)(2,1)S(1)}, u32[]{:S(2)}, u32[]{:S(2)}) collective-permute-start(bf16[1552,128]{1,0:T(8,128)(2,1)S(1)} %get-tuple-element.63.mine), channel_id=1, source_target_pairs={{0,8},{1,9},{2,10},{3,11},{4,12},{5,13},{6,14},{7,15},{8,0},{9,1},... | collective-permute-start | bytes 1191944 | tf_op jit(solution)/shard_map/ppermute | solution.py:453
  26.7 5.5 %collective-permute-start.9 = (bf16[512,128]{1,0:T(8,128)(2,1)S(1)}, bf16[512,128]{1,0:T(8,128)(2,1)S(1)}, u32[]{:S(2)}, u32[]{:S(2)}) collective-permute-start(bf16[512,128]{1,0:T(8,128)(2,1)S(1)} %get-tuple-element.59), channel_id=1, source_target_pairs={{0,2},{1,3},{2,0},{3,1},{4,6},{5,7},{6,4},{7,5},{8,10},{9,11},{10,... | collective-permute-start | bytes 393224 | tf_op jit(solution)/shard_map/ppermute | solution.py:453
  27.3 11.1 %collective-permute-start.10 = (bf16[512,128]{1,0:T(8,128)(2,1)S(1)}, bf16[512,128]{1,0:T(8,128)(2,1)S(1)}, u32[]{:S(2)}, u32[]{:S(2)}) collective-permute-start(bf16[512,128]{1,0:T(8,128)(2,1)S(1)} %get-tuple-element.60), channel_id=1, source_target_pairs={{0,4},{1,5},{2,6},{3,7},{4,0},{5,1},{6,2},{7,3},{8,12},{9,13},{10,... | collective-permute-start | bytes 393224 | tf_op jit(solution)/shard_map/ppermute | solution.py:453
  28.8 11.8 %collective-permute-start.11 = (bf16[512,128]{1,0:T(8,128)(2,1)S(1)}, bf16[512,128]{1,0:T(8,128)(2,1)S(1)}, u32[]{:S(2)}, u32[]{:S(2)}) collective-permute-start(bf16[512,128]{1,0:T(8,128)(2,1)S(1)} %get-tuple-element.61), channel_id=1, source_target_pairs={{0,6},{1,7},{2,4},{3,5},{4,2},{5,3},{6,0},{7,1},{8,14},{9,15},{10,... | collective-permute-start | bytes 393224 | tf_op jit(solution)/shard_map/ppermute | solution.py:453
  40.7 1.6 %collective-permute-start.12 = (bf16[1024,128]{1,0:T(8,128)(2,1)S(1)}, bf16[1024,128]{1,0:T(8,128)(2,1)S(1)}, u32[]{:S(2)}, u32[]{:S(2)}) collective-permute-start(bf16[1024,128]{1,0:T(8,128)(2,1)S(1)} %for_mate.2), channel_id=1, source_target_pairs={{0,1},{1,0},{2,3},{3,2},{4,5},{5,4},{6,7},{7,6},{8,9},{9,8},{10,11... | collective-permute-start | bytes 786440 | tf_op jit(solution)/shard_map/ppermute | solution.py:453
  47.0 20.2 %collective-permute-start.18 = (bf16[1536,128]{1,0:T(8,128)(2,1)}, bf16[1536,128]{1,0:T(8,128)(2,1)S(1)}, u32[]{:S(2)}, u32[]{:S(2)}) collective-permute-start(bf16[1536,128]{1,0:T(8,128)(2,1)} %get-tuple-element.74), channel_id=1, source_target_pairs={{0,8},{1,9},{2,10},{3,11},{4,12},{5,13},{6,14},{7,15},{8,0},{9,1},... | collective-permute-start | bytes 1179656 | tf_op jit(solution)/shard_map/ppermute | solution.py:453
  47.3 5.3 %collective-permute-start.14 = (bf16[512,128]{1,0:T(8,128)(2,1)S(1)}, bf16[512,128]{1,0:T(8,128)(2,1)S(1)}, u32[]{:S(2)}, u32[]{:S(2)}) collective-permute-start(bf16[512,128]{1,0:T(8,128)(2,1)S(1)} %get-tuple-element.66), channel_id=1, source_target_pairs={{0,2},{1,3},{2,0},{3,1},{4,6},{5,7},{6,4},{7,5},{8,10},{9,11},{10,... | collective-permute-start | bytes 393224 | tf_op jit(solution)/shard_map/ppermute | solution.py:453
  48.8 11.0 %collective-permute-start.15 = (bf16[512,128]{1,0:T(8,128)(2,1)S(1)}, bf16[512,128]{1,0:T(8,128)(2,1)S(1)}, u32[]{:S(2)}, u32[]{:S(2)}) collective-permute-start(bf16[512,128]{1,0:T(8,128)(2,1)S(1)} %get-tuple-element.67), channel_id=1, source_target_pairs={{0,4},{1,5},{2,6},{3,7},{4,0},{5,1},{6,2},{7,3},{8,12},{9,13},{10,... | collective-permute-start | bytes 393224 | tf_op jit(solution)/shard_map/ppermute | solution.py:453
  51.6 10.3 %collective-permute-start.16 = (bf16[512,128]{1,0:T(8,128)(2,1)S(1)}, bf16[512,128]{1,0:T(8,128)(2,1)S(1)}, u32[]{:S(2)}, u32[]{:S(2)}) collective-permute-start(bf16[512,128]{1,0:T(8,128)(2,1)S(1)} %get-tuple-element.68), channel_id=1, source_target_pairs={{0,6},{1,7},{2,4},{3,5},{4,2},{5,3},{6,0},{7,1},{8,14},{9,15},{10,... | collective-permute-start | bytes 393224 | tf_op jit(solution)/shard_map/ppermute | solution.py:453
  61.9 7.6 %collective-permute-start.17 = (bf16[1024,128]{1,0:T(8,128)(2,1)S(1)}, bf16[1024,128]{1,0:T(8,128)(2,1)S(1)}, u32[]{:S(2)}, u32[]{:S(2)}) collective-permute-start(bf16[1024,128]{1,0:T(8,128)(2,1)S(1)} %for_mate.3), channel_id=1, source_target_pairs={{0,1},{1,0},{2,3},{3,2},{4,5},{5,4},{6,7},{7,6},{8,9},{9,8},{10,11... | collective-permute-start | bytes 786440 | tf_op jit(solution)/shard_map/ppermute | solution.py:453
  67.6 3.6 %collective-permute-start.21 = (bf16[512,128]{1,0:T(8,128)(2,1)S(1)}, bf16[512,128]{1,0:T(8,128)(2,1)S(1)}, u32[]{:S(2)}, u32[]{:S(2)}) collective-permute-start(bf16[512,128]{1,0:T(8,128)(2,1)S(1)} %get-tuple-element.79), channel_id=1, source_target_pairs={{0,1},{1,0},{2,3},{3,2},{4,5},{5,4},{6,7},{7,6},{8,9},{9,8},{10,11... | collective-permute-start | bytes 393224 | tf_op jit(solution)/shard_map/ppermute | solution.py:453
  67.7 6.4 %collective-permute-start.22 = (bf16[512,128]{1,0:T(8,128)(2,1)S(1)}, bf16[512,128]{1,0:T(8,128)(2,1)S(1)}, u32[]{:S(2)}, u32[]{:S(2)}) collective-permute-start(bf16[512,128]{1,0:T(8,128)(2,1)S(1)} %get-tuple-element.80), channel_id=1, source_target_pairs={{0,2},{1,3},{2,0},{3,1},{4,6},{5,7},{6,4},{7,5},{8,10},{9,11},{10,... | collective-permute-start | bytes 393224 | tf_op jit(solution)/shard_map/ppermute | solution.py:453
  68.3 7.6 %collective-permute-start.23 = (bf16[512,128]{1,0:T(8,128)(2,1)S(1)}, bf16[512,128]{1,0:T(8,128)(2,1)S(1)}, u32[]{:S(2)}, u32[]{:S(2)}) collective-permute-start(bf16[512,128]{1,0:T(8,128)(2,1)S(1)} %get-tuple-element.81), channel_id=1, source_target_pairs={{0,3},{1,2},{2,1},{3,0},{4,7},{5,6},{6,5},{7,4},{8,11},{9,10},{10,... | collective-permute-start | bytes 393224 | tf_op jit(solution)/shard_map/ppermute | solution.py:453
  69.6 6.4 %collective-permute-start.24 = (bf16[512,128]{1,0:T(8,128)(2,1)S(1)}, bf16[512,128]{1,0:T(8,128)(2,1)S(1)}, u32[]{:S(2)}, u32[]{:S(2)}) collective-permute-start(bf16[512,128]{1,0:T(8,128)(2,1)S(1)} %get-tuple-element.82), channel_id=1, source_target_pairs={{0,4},{1,5},{2,6},{3,7},{4,0},{5,1},{6,2},{7,3},{8,12},{9,13},{10,... | collective-permute-start | bytes 393224 | tf_op jit(solution)/shard_map/ppermute | solution.py:453
  69.6 8.0 %collective-permute-start.25 = (bf16[512,128]{1,0:T(8,128)(2,1)S(1)}, bf16[512,128]{1,0:T(8,128)(2,1)S(1)}, u32[]{:S(2)}, u32[]{:S(2)}) collective-permute-start(bf16[512,128]{1,0:T(8,128)(2,1)S(1)} %get-tuple-element.83), channel_id=1, source_target_pairs={{0,5},{1,4},{2,7},{3,6},{4,1},{5,0},{6,3},{7,2},{8,13},{9,12},{10,... | collective-permute-start | bytes 393224 | tf_op jit(solution)/shard_map/ppermute | solution.py:453
  71.3 10.3 %collective-permute-start.19 = (bf16[512,128]{1,0:T(8,128)(2,1)S(1)}, bf16[512,128]{1,0:T(8,128)(2,1)S(1)}, u32[]{:S(2)}, u32[]{:S(2)}) collective-permute-start(bf16[512,128]{1,0:T(8,128)(2,1)S(1)} %get-tuple-element.76), channel_id=1, source_target_pairs={{0,6},{1,7},{2,4},{3,5},{4,2},{5,3},{6,0},{7,1},{8,14},{9,15},{10,... | collective-permute-start | bytes 393224 | tf_op jit(solution)/shard_map/ppermute | solution.py:453
  74.1 9.1 %collective-permute-start.20 = (bf16[512,128]{1,0:T(8,128)(2,1)S(1)}, bf16[512,128]{1,0:T(8,128)(2,1)S(1)}, u32[]{:S(2)}, u32[]{:S(2)}) collective-permute-start(bf16[512,128]{1,0:T(8,128)(2,1)S(1)} %get-tuple-element.77), channel_id=1, source_target_pairs={{0,7},{1,6},{2,5},{3,4},{4,3},{5,2},{6,1},{7,0},{8,15},{9,14},{10,... | collective-permute-start | bytes 393224 | tf_op jit(solution)/shard_map/ppermute | solution.py:453
  (5 other events, 16.1 us)

commit v4 on v3

--- a/solution.py
+++ b/solution.py
@@ -569,7 +569,7 @@
     )(hot, rounded, *got)
     got = in_group(out)
     gradient = []
-    for members in (range(GROUP - 2), range(GROUP - 2, GROUP)):
+    for members in (range(GROUP - 2), range(GROUP - 2, GROUP - 1), range(GROUP - 1, GROUP)):
         rows = len(members) * block // GROUP
         gradient = [
             call(

time: 84.6 us -> 84.5 us (level)
  waiting for transfers between devices: 44.4 us -> 43.3 us
  Pallas kernels: 11 us -> 12.1 us
    ppermute x24, waiting for transfers between devices: 44.4 us -> 43.3 us  [swap(): lax.ppermute(value, 'tiles', [(i, i ^ distance) for i in range(peers)])]
    pallas_call x2 -> x3, Pallas kernels: 2.87 us -> 3.94 us  [per_device(): call(functools.partial(gradient_kernel, members), 'gradient', in_hbm(tile...]
  transfers between devices with their start and end apart: 24 -> 24, of which waited for: 18 -> 18; matrix products, arithmetic and copies ran while one was open for 1% -> 1% of each run, Pallas kernels for 5% -> 6%
where the time goes in v4:
time: 84.5 us; the launch traced here: 84.3 us
  waiting for transfers between devices  43.3 us (51%)
  starting transfers between devices  25.3 us (30%)
  Pallas kernels  12.1 us (14%)
  local copies, waits for them, and re-layouts  2.15 us (3%)
  between operations  1.42 us (2%)
    ppermute x24, waiting for transfers between devices, swap(): lax.ppermute(value, 'tiles', [(i, i ^ distance) for i in range(peers)])  43.3 us
    ppermute x24, starting transfers between devices, swap(): lax.ppermute(value, 'tiles', [(i, i ^ distance) for i in range(peers)])  25.3 us
    pallas_call x3, Pallas kernels, per_device(): call(functools.partial(gradient_kernel, members), 'gradient', in_hbm(tile...  3.94 us
    pallas_call x1, Pallas kernels, per_device(): call(parts_kernel, 'parts', [in_hbm(shape(freq_count, 2, block)), in_hbm(...  2.67 us
    pallas_call x1, Pallas kernels, per_device(): call(functools.partial(residual_kernel, sizes), 'residual_slices', [shape...  1.86 us
  transfers between devices with their start and end apart: 24, of which 18 were waited for; matrix products, arithmetic and copies ran while one was open for 1% of the time, Pallas kernels for 6%

profile of v4, /device:TPU:0, one launch (start us, length us, event | category | flops | bytes accessed | tf_op | source)
XLA Modules:
  0.0 84.3 jit_solution(14608525165622442556)
XLA Ops:
  1.3 2.7 %parts.1 = (bf16[8,2,128,128]{3,2,1,0:T(8,128)(2,1)}, bf16[256,128]{1,0:T(8,128)(2,1)}, s32[16]{0:T(128)S(4)}, bf16[528,128]{1,0:T(8,128)(2,1)S(1)}, bf16[528,12...) custom-call(bf16[8,2,128,128]{3,2,1,0:T(8,128)(2,1)} %data.3, ...), custom_call_target="tpu_custom_call" | custom-call | bytes 1048576 | tf_op jit(solution)/shard_map/parts/pallas_call | solution.py:469
  4.5 2.6 %collective-permute-start.3 = (bf16[528,128]{1,0:T(8,128)(2,1)S(1)}, bf16[528,128]{1,0:T(8,128)(2,1)S(1)}, u32[]{:S(2)}, u32[]{:S(2)}) collective-permute-start(bf16[528,128]{1,0:T(8,128)(2,1)S(1)} %get-tuple-element.49), channel_id=1, source_target_pairs={{0,2},{1,3},{2,0},{3,1},{4,6},{5,7},{6,4},{7,5},{8,10},{9,11},{10,... | collective-permute-start | bytes 405512 | tf_op jit(solution)/shard_map/ppermute | solution.py:453
  7.1 1.8 %collective-permute-start.5 = (bf16[528,128]{1,0:T(8,128)(2,1)S(1)}, bf16[528,128]{1,0:T(8,128)(2,1)S(1)}, u32[]{:S(2)}, u32[]{:S(2)}) collective-permute-start(bf16[528,128]{1,0:T(8,128)(2,1)S(1)} %get-tuple-element.51), channel_id=1, source_target_pairs={{0,4},{1,5},{2,6},{3,7},{4,0},{5,1},{6,2},{7,3},{8,12},{9,13},{10,... | collective-permute-start | bytes 405512 | tf_op jit(solution)/shard_map/ppermute | solution.py:453
  8.9 2.6 %collective-permute-start.7 = (bf16[528,128]{1,0:T(8,128)(2,1)S(1)}, bf16[528,128]{1,0:T(8,128)(2,1)S(1)}, u32[]{:S(2)}, u32[]{:S(2)}) collective-permute-start(bf16[528,128]{1,0:T(8,128)(2,1)S(1)} %get-tuple-element.53), channel_id=1, source_target_pairs={{0,6},{1,7},{2,4},{3,5},{4,2},{5,3},{6,0},{7,1},{8,14},{9,15},{10,... | collective-permute-start | bytes 405512 | tf_op jit(solution)/shard_map/ppermute | solution.py:453
  11.6 1.7 %collective-permute-start.8 = (bf16[528,128]{1,0:T(8,128)(2,1)S(1)}, bf16[528,128]{1,0:T(8,128)(2,1)S(1)}, u32[]{:S(2)}, u32[]{:S(2)}) collective-permute-start(bf16[528,128]{1,0:T(8,128)(2,1)S(1)} %get-tuple-element.54), channel_id=1, source_target_pairs={{0,7},{1,6},{2,5},{3,4},{4,3},{5,2},{6,1},{7,0},{8,15},{9,14},{10,... | collective-permute-start | bytes 405512 | tf_op jit(solution)/shard_map/ppermute | solution.py:453
  13.9 1.9 %collective-permute-done.6.refs_5_ = bf16[528,128]{1,0:T(8,128)(2,1)S(1)} collective-permute-done((bf16[528,128]{1,0:T(8,128)(2,1)S(1)}, bf16[528,128]{1,0:T(8,128)(2,1)S(1)}, u32[]{:S(2)}, u32[]{:S(2)}) %collective-permute-start.6) | collective-permute-done | bytes 135200 | tf_op jit(solution)/shard_map/ppermute | solution.py:453
  15.8 4.7 %collective-permute-done.7.refs_6_ = bf16[528,128]{1,0:T(8,128)(2,1)S(1)} collective-permute-done((bf16[528,128]{1,0:T(8,128)(2,1)S(1)}, bf16[528,128]{1,0:T(8,128)(2,1)S(1)}, u32[]{:S(2)}, u32[]{:S(2)}) %collective-permute-start.7) | collective-permute-done | bytes 135200 | tf_op jit(solution)/shard_map/ppermute | solution.py:453
  20.5 1.8 %collective-permute-done.8.refs_7_ = bf16[528,128]{1,0:T(8,128)(2,1)S(1)} collective-permute-done((bf16[528,128]{1,0:T(8,128)(2,1)S(1)}, bf16[528,128]{1,0:T(8,128)(2,1)S(1)}, u32[]{:S(2)}, u32[]{:S(2)}) %collective-permute-start.8) | collective-permute-done | bytes 135200 | tf_op jit(solution)/shard_map/ppermute | solution.py:453
  23.3 2.7 %collective-permute-start.13 = (bf16[1552,128]{1,0:T(8,128)(2,1)S(1)}, bf16[1552,128]{1,0:T(8,128)(2,1)S(1)}, u32[]{:S(2)}, u32[]{:S(2)}) collective-permute-start(bf16[1552,128]{1,0:T(8,128)(2,1)S(1)} %get-tuple-element.63.mine), channel_id=1, source_target_pairs={{0,8},{1,9},{2,10},{3,11},{4,12},{5,13},{6,14},{7,15},{8,0},{9,1},... | collective-permute-start | bytes 1191944 | tf_op jit(solution)/shard_map/ppermute | solution.py:453
  27.3 1.6 %collective-permute-start.10 = (bf16[512,128]{1,0:T(8,128)(2,1)S(1)}, bf16[512,128]{1,0:T(8,128)(2,1)S(1)}, u32[]{:S(2)}, u32[]{:S(2)}) collective-permute-start(bf16[512,128]{1,0:T(8,128)(2,1)S(1)} %get-tuple-element.60), channel_id=1, source_target_pairs={{0,4},{1,5},{2,6},{3,7},{4,0},{5,1},{6,2},{7,3},{8,12},{9,13},{10,... | collective-permute-start | bytes 393224 | tf_op jit(solution)/shard_map/ppermute | solution.py:453
  30.2 2.0 %collective-permute-done.9.refs_0_.refs_1_ = bf16[512,128]{1,0:T(8,128)(2,1)S(1)} collective-permute-done((bf16[512,128]{1,0:T(8,128)(2,1)S(1)}, bf16[512,128]{1,0:T(8,128)(2,1)S(1)}, u32[]{:S(2)}, u32[]{:S(2)}) %collective-permute-start.9) | collective-permute-done | bytes 131104 | tf_op jit(solution)/shard_map/ppermute | solution.py:453
  32.2 6.1 %collective-permute-done.10.refs_1_.refs_2_ = bf16[512,128]{1,0:T(8,128)(2,1)S(1)} collective-permute-done((bf16[512,128]{1,0:T(8,128)(2,1)S(1)}, bf16[512,128]{1,0:T(8,128)(2,1)S(1)}, u32[]{:S(2)}, u32[]{:S(2)}) %collective-permute-start.10) | collective-permute-done | bytes 131104 | tf_op jit(solution)/shard_map/ppermute | solution.py:453
  38.4 2.3 %collective-permute-done.11.refs_2_.refs_3_ = bf16[512,128]{1,0:T(8,128)(2,1)S(1)} collective-permute-done((bf16[512,128]{1,0:T(8,128)(2,1)S(1)}, bf16[512,128]{1,0:T(8,128)(2,1)S(1)}, u32[]{:S(2)}, u32[]{:S(2)}) %collective-permute-start.11) | collective-permute-done | bytes 131104 | tf_op jit(solution)/shard_map/ppermute | solution.py:453
  42.3 2.0 %collective-permute-done.13.got.refs_6_ = bf16[1552,128]{1,0:T(8,128)(2,1)S(1)} collective-permute-done((bf16[1552,128]{1,0:T(8,128)(2,1)S(1)}, bf16[1552,128]{1,0:T(8,128)(2,1)S(1)}, u32[]{:S(2)}, u32[]{:S(2)}) %collective-permute-start.13) | collective-permute-done | bytes 397344 | tf_op jit(solution)/shard_map/ppermute | solution.py:453
  45.1 1.9 %residual_slices.1 = (bf16[32,64,128]{2,1,0:T(8,128)(2,1)S(1)}, bf16[1536,128]{1,0:T(8,128)(2,1)}, bf16[32,16,128]{2,1,0:T(8,128)(2,1)}, bf16[256,128]{1,0:T(8,1...) custom-call(f32[32,64,128]{2,1,0:T(8,128)S(1)} %get-tuple-element.55, ...), custom_call_target="tpu_custom_call" | custom-call | bytes 1048576 | tf_op jit(solution)/shard_map/residual_slices/pallas_call | solution.py:532
  48.8 2.7 %collective-permute-start.15 = (bf16[512,128]{1,0:T(8,128)(2,1)S(1)}, bf16[512,128]{1,0:T(8,128)(2,1)S(1)}, u32[]{:S(2)}, u32[]{:S(2)}) collective-permute-start(bf16[512,128]{1,0:T(8,128)(2,1)S(1)} %get-tuple-element.67), channel_id=1, source_target_pairs={{0,4},{1,5},{2,6},{3,7},{4,0},{5,1},{6,2},{7,3},{8,12},{9,13},{10,... | collective-permute-start | bytes 393224 | tf_op jit(solution)/shard_map/ppermute | solution.py:453
  52.6 7.3 %collective-permute-done.15.refs_1_.refs_2_ = bf16[512,128]{1,0:T(8,128)(2,1)S(1)} collective-permute-done((bf16[512,128]{1,0:T(8,128)(2,1)S(1)}, bf16[512,128]{1,0:T(8,128)(2,1)S(1)}, u32[]{:S(2)}, u32[]{:S(2)}) %collective-permute-start.15) | collective-permute-done | bytes 131104 | tf_op jit(solution)/shard_map/ppermute | solution.py:453
  59.9 2.0 %collective-permute-done.16.refs_2_.refs_3_ = bf16[512,128]{1,0:T(8,128)(2,1)S(1)} collective-permute-done((bf16[512,128]{1,0:T(8,128)(2,1)S(1)}, bf16[512,128]{1,0:T(8,128)(2,1)S(1)}, u32[]{:S(2)}, u32[]{:S(2)}) %collective-permute-start.16) | collective-permute-done | bytes 131104 | tf_op jit(solution)/shard_map/ppermute | solution.py:453
  63.5 3.7 %collective-permute-done.18.refs_1_ = bf16[1536,128]{1,0:T(8,128)(2,1)S(1)} collective-permute-done((bf16[1536,128]{1,0:T(8,128)(2,1)}, bf16[1536,128]{1,0:T(8,128)(2,1)S(1)}, u32[]{:S(2)}, u32[]{:S(2)}) %collective-permute-start.18) | collective-permute-done | bytes 393248 | tf_op jit(solution)/shard_map/ppermute | solution.py:453
  69.6 1.7 %collective-permute-start.25 = (bf16[512,128]{1,0:T(8,128)(2,1)S(1)}, bf16[512,128]{1,0:T(8,128)(2,1)S(1)}, u32[]{:S(2)}, u32[]{:S(2)}) collective-permute-start(bf16[512,128]{1,0:T(8,128)(2,1)S(1)} %get-tuple-element.83), channel_id=1, source_target_pairs={{0,5},{1,4},{2,7},{3,6},{4,1},{5,0},{6,3},{7,2},{8,13},{9,12},{10,... | collective-permute-start | bytes 393224 | tf_op jit(solution)/shard_map/ppermute | solution.py:453
  71.7 2.4 %collective-permute-done.22.refs_2_ = bf16[512,128]{1,0:T(8,128)(2,1)S(1)} collective-permute-done((bf16[512,128]{1,0:T(8,128)(2,1)S(1)}, bf16[512,128]{1,0:T(8,128)(2,1)S(1)}, u32[]{:S(2)}, u32[]{:S(2)}) %collective-permute-start.22) | collective-permute-done | bytes 131104 | tf_op jit(solution)/shard_map/ppermute | solution.py:453
  76.0 1.6 %collective-permute-done.25.refs_5_ = bf16[512,128]{1,0:T(8,128)(2,1)S(1)} collective-permute-done((bf16[512,128]{1,0:T(8,128)(2,1)S(1)}, bf16[512,128]{1,0:T(8,128)(2,1)S(1)}, u32[]{:S(2)}, u32[]{:S(2)}) %collective-permute-start.25) | collective-permute-done | bytes 131104 | tf_op jit(solution)/shard_map/ppermute | solution.py:453
  77.5 1.7 %gradient.3.refs_1_ = bf16[16,2,128,128]{3,2,1,0:T(8,128)(2,1)} custom-call(bf16[8,2,128,128]{3,2,1,0:T(8,128)(2,1)S(1)} %copy-done.1, s32[16]{0:T(128)S(4)} %get-tuple-element.71.freqs, bf16[512,128]{1,0:T(8,128)(2,1)S(1)} %get-tuple-element.78.refs_0_, bf16[512,128]{1,0:T(8,128)(2,1)S(1)} %collective-permute-done.21.refs_1_, ...), custom_call_target="tpu_custom_call" | custom-call | bytes 1048576 | tf_op jit(solution)/shard_map/gradient/pallas_call | solution.py:575
  79.2 2.3 %collective-permute-done.20.refs_0_ = bf16[512,128]{1,0:T(8,128)(2,1)S(1)} collective-permute-done((bf16[512,128]{1,0:T(8,128)(2,1)S(1)}, bf16[512,128]{1,0:T(8,128)(2,1)S(1)}, u32[]{:S(2)}, u32[]{:S(2)}) %collective-permute-start.20) | collective-permute-done | bytes 131104 | tf_op jit(solution)/shard_map/ppermute | solution.py:453
  (50 shorter events, 20.6 us)
Async XLA Ops:
  4.0 5.0 %collective-permute-start.2 = (bf16[528,128]{1,0:T(8,128)(2,1)S(1)}, bf16[528,128]{1,0:T(8,128)(2,1)S(1)}, u32[]{:S(2)}, u32[]{:S(2)}) collective-permute-start(bf16[528,128]{1,0:T(8,128)(2,1)S(1)} %get-tuple-element.48), channel_id=1, source_target_pairs={{0,1},{1,0},{2,3},{3,2},{4,5},{5,4},{6,7},{7,6},{8,9},{9,8},{10,11... | collective-permute-start | bytes 405512 | tf_op jit(solution)/shard_map/ppermute | solution.py:453
  4.5 7.1 %collective-permute-start.3 = (bf16[528,128]{1,0:T(8,128)(2,1)S(1)}, bf16[528,128]{1,0:T(8,128)(2,1)S(1)}, u32[]{:S(2)}, u32[]{:S(2)}) collective-permute-start(bf16[528,128]{1,0:T(8,128)(2,1)S(1)} %get-tuple-element.49), channel_id=1, source_target_pairs={{0,2},{1,3},{2,0},{3,1},{4,6},{5,7},{6,4},{7,5},{8,10},{9,11},{10,... | collective-permute-start | bytes 405512 | tf_op jit(solution)/shard_map/ppermute | solution.py:453
  7.1 6.8 %collective-permute-start.4 = (bf16[528,128]{1,0:T(8,128)(2,1)S(1)}, bf16[528,128]{1,0:T(8,128)(2,1)S(1)}, u32[]{:S(2)}, u32[]{:S(2)}) collective-permute-start(bf16[528,128]{1,0:T(8,128)(2,1)S(1)} %get-tuple-element.50), channel_id=1, source_target_pairs={{0,3},{1,2},{2,1},{3,0},{4,7},{5,6},{6,5},{7,4},{8,11},{9,10},{10,... | collective-permute-start | bytes 405512 | tf_op jit(solution)/shard_map/ppermute | solution.py:453
  7.1 6.7 %collective-permute-start.5 = (bf16[528,128]{1,0:T(8,128)(2,1)S(1)}, bf16[528,128]{1,0:T(8,128)(2,1)S(1)}, u32[]{:S(2)}, u32[]{:S(2)}) collective-permute-start(bf16[528,128]{1,0:T(8,128)(2,1)S(1)} %get-tuple-element.51), channel_id=1, source_target_pairs={{0,4},{1,5},{2,6},{3,7},{4,0},{5,1},{6,2},{7,3},{8,12},{9,13},{10,... | collective-permute-start | bytes 405512 | tf_op jit(solution)/shard_map/ppermute | solution.py:453
  8.9 6.8 %collective-permute-start.6 = (bf16[528,128]{1,0:T(8,128)(2,1)S(1)}, bf16[528,128]{1,0:T(8,128)(2,1)S(1)}, u32[]{:S(2)}, u32[]{:S(2)}) collective-permute-start(bf16[528,128]{1,0:T(8,128)(2,1)S(1)} %get-tuple-element.52), channel_id=1, source_target_pairs={{0,5},{1,4},{2,7},{3,6},{4,1},{5,0},{6,3},{7,2},{8,13},{9,12},{10,... | collective-permute-start | bytes 405512 | tf_op jit(solution)/shard_map/ppermute | solution.py:453
  8.9 11.5 %collective-permute-start.7 = (bf16[528,128]{1,0:T(8,128)(2,1)S(1)}, bf16[528,128]{1,0:T(8,128)(2,1)S(1)}, u32[]{:S(2)}, u32[]{:S(2)}) collective-permute-start(bf16[528,128]{1,0:T(8,128)(2,1)S(1)} %get-tuple-element.53), channel_id=1, source_target_pairs={{0,6},{1,7},{2,4},{3,5},{4,2},{5,3},{6,0},{7,1},{8,14},{9,15},{10,... | collective-permute-start | bytes 405512 | tf_op jit(solution)/shard_map/ppermute | solution.py:453
  11.6 10.7 %collective-permute-start.8 = (bf16[528,128]{1,0:T(8,128)(2,1)S(1)}, bf16[528,128]{1,0:T(8,128)(2,1)S(1)}, u32[]{:S(2)}, u32[]{:S(2)}) collective-permute-start(bf16[528,128]{1,0:T(8,128)(2,1)S(1)} %get-tuple-element.54), channel_id=1, source_target_pairs={{0,7},{1,6},{2,5},{3,4},{4,3},{5,2},{6,1},{7,0},{8,15},{9,14},{10,... | collective-permute-start | bytes 405512 | tf_op jit(solution)/shard_map/ppermute | solution.py:453
  23.3 21.0 %collective-permute-start.13 = (bf16[1552,128]{1,0:T(8,128)(2,1)S(1)}, bf16[1552,128]{1,0:T(8,128)(2,1)S(1)}, u32[]{:S(2)}, u32[]{:S(2)}) collective-permute-start(bf16[1552,128]{1,0:T(8,128)(2,1)S(1)} %get-tuple-element.63.mine), channel_id=1, source_target_pairs={{0,8},{1,9},{2,10},{3,11},{4,12},{5,13},{6,14},{7,15},{8,0},{9,1},... | collective-permute-start | bytes 1191944 | tf_op jit(solution)/shard_map/ppermute | solution.py:453
  26.7 5.5 %collective-permute-start.9 = (bf16[512,128]{1,0:T(8,128)(2,1)S(1)}, bf16[512,128]{1,0:T(8,128)(2,1)S(1)}, u32[]{:S(2)}, u32[]{:S(2)}) collective-permute-start(bf16[512,128]{1,0:T(8,128)(2,1)S(1)} %get-tuple-element.59), channel_id=1, source_target_pairs={{0,2},{1,3},{2,0},{3,1},{4,6},{5,7},{6,4},{7,5},{8,10},{9,11},{10,... | collective-permute-start | bytes 393224 | tf_op jit(solution)/shard_map/ppermute | solution.py:453
  27.3 11.1 %collective-permute-start.10 = (bf16[512,128]{1,0:T(8,128)(2,1)S(1)}, bf16[512,128]{1,0:T(8,128)(2,1)S(1)}, u32[]{:S(2)}, u32[]{:S(2)}) collective-permute-start(bf16[512,128]{1,0:T(8,128)(2,1)S(1)} %get-tuple-element.60), channel_id=1, source_target_pairs={{0,4},{1,5},{2,6},{3,7},{4,0},{5,1},{6,2},{7,3},{8,12},{9,13},{10,... | collective-permute-start | bytes 393224 | tf_op jit(solution)/shard_map/ppermute | solution.py:453
  28.8 11.8 %collective-permute-start.11 = (bf16[512,128]{1,0:T(8,128)(2,1)S(1)}, bf16[512,128]{1,0:T(8,128)(2,1)S(1)}, u32[]{:S(2)}, u32[]{:S(2)}) collective-permute-start(bf16[512,128]{1,0:T(8,128)(2,1)S(1)} %get-tuple-element.61), channel_id=1, source_target_pairs={{0,6},{1,7},{2,4},{3,5},{4,2},{5,3},{6,0},{7,1},{8,14},{9,15},{10,... | collective-permute-start | bytes 393224 | tf_op jit(solution)/shard_map/ppermute | solution.py:453
  40.7 1.6 %collective-permute-start.12 = (bf16[1024,128]{1,0:T(8,128)(2,1)S(1)}, bf16[1024,128]{1,0:T(8,128)(2,1)S(1)}, u32[]{:S(2)}, u32[]{:S(2)}) collective-permute-start(bf16[1024,128]{1,0:T(8,128)(2,1)S(1)} %for_mate.2), channel_id=1, source_target_pairs={{0,1},{1,0},{2,3},{3,2},{4,5},{5,4},{6,7},{7,6},{8,9},{9,8},{10,11... | collective-permute-start | bytes 786440 | tf_op jit(solution)/shard_map/ppermute | solution.py:453
  47.0 20.2 %collective-permute-start.18 = (bf16[1536,128]{1,0:T(8,128)(2,1)}, bf16[1536,128]{1,0:T(8,128)(2,1)S(1)}, u32[]{:S(2)}, u32[]{:S(2)}) collective-permute-start(bf16[1536,128]{1,0:T(8,128)(2,1)} %get-tuple-element.74), channel_id=1, source_target_pairs={{0,8},{1,9},{2,10},{3,11},{4,12},{5,13},{6,14},{7,15},{8,0},{9,1},... | collective-permute-start | bytes 1179656 | tf_op jit(solution)/shard_map/ppermute | solution.py:453
  47.3 5.3 %collective-permute-start.14 = (bf16[512,128]{1,0:T(8,128)(2,1)S(1)}, bf16[512,128]{1,0:T(8,128)(2,1)S(1)}, u32[]{:S(2)}, u32[]{:S(2)}) collective-permute-start(bf16[512,128]{1,0:T(8,128)(2,1)S(1)} %get-tuple-element.66), channel_id=1, source_target_pairs={{0,2},{1,3},{2,0},{3,1},{4,6},{5,7},{6,4},{7,5},{8,10},{9,11},{10,... | collective-permute-start | bytes 393224 | tf_op jit(solution)/shard_map/ppermute | solution.py:453
  48.8 11.0 %collective-permute-start.15 = (bf16[512,128]{1,0:T(8,128)(2,1)S(1)}, bf16[512,128]{1,0:T(8,128)(2,1)S(1)}, u32[]{:S(2)}, u32[]{:S(2)}) collective-permute-start(bf16[512,128]{1,0:T(8,128)(2,1)S(1)} %get-tuple-element.67), channel_id=1, source_target_pairs={{0,4},{1,5},{2,6},{3,7},{4,0},{5,1},{6,2},{7,3},{8,12},{9,13},{10,... | collective-permute-start | bytes 393224 | tf_op jit(solution)/shard_map/ppermute | solution.py:453
  51.6 10.3 %collective-permute-start.16 = (bf16[512,128]{1,0:T(8,128)(2,1)S(1)}, bf16[512,128]{1,0:T(8,128)(2,1)S(1)}, u32[]{:S(2)}, u32[]{:S(2)}) collective-permute-start(bf16[512,128]{1,0:T(8,128)(2,1)S(1)} %get-tuple-element.68), channel_id=1, source_target_pairs={{0,6},{1,7},{2,4},{3,5},{4,2},{5,3},{6,0},{7,1},{8,14},{9,15},{10,... | collective-permute-start | bytes 393224 | tf_op jit(solution)/shard_map/ppermute | solution.py:453
  61.9 7.6 %collective-permute-start.17 = (bf16[1024,128]{1,0:T(8,128)(2,1)S(1)}, bf16[1024,128]{1,0:T(8,128)(2,1)S(1)}, u32[]{:S(2)}, u32[]{:S(2)}) collective-permute-start(bf16[1024,128]{1,0:T(8,128)(2,1)S(1)} %for_mate.3), channel_id=1, source_target_pairs={{0,1},{1,0},{2,3},{3,2},{4,5},{5,4},{6,7},{7,6},{8,9},{9,8},{10,11... | collective-permute-start | bytes 786440 | tf_op jit(solution)/shard_map/ppermute | solution.py:453
  67.6 3.6 %collective-permute-start.21 = (bf16[512,128]{1,0:T(8,128)(2,1)S(1)}, bf16[512,128]{1,0:T(8,128)(2,1)S(1)}, u32[]{:S(2)}, u32[]{:S(2)}) collective-permute-start(bf16[512,128]{1,0:T(8,128)(2,1)S(1)} %get-tuple-element.79), channel_id=1, source_target_pairs={{0,1},{1,0},{2,3},{3,2},{4,5},{5,4},{6,7},{7,6},{8,9},{9,8},{10,11... | collective-permute-start | bytes 393224 | tf_op jit(solution)/shard_map/ppermute | solution.py:453
  67.7 6.4 %collective-permute-start.22 = (bf16[512,128]{1,0:T(8,128)(2,1)S(1)}, bf16[512,128]{1,0:T(8,128)(2,1)S(1)}, u32[]{:S(2)}, u32[]{:S(2)}) collective-permute-start(bf16[512,128]{1,0:T(8,128)(2,1)S(1)} %get-tuple-element.80), channel_id=1, source_target_pairs={{0,2},{1,3},{2,0},{3,1},{4,6},{5,7},{6,4},{7,5},{8,10},{9,11},{10,... | collective-permute-start | bytes 393224 | tf_op jit(solution)/shard_map/ppermute | solution.py:453
  68.3 7.6 %collective-permute-start.23 = (bf16[512,128]{1,0:T(8,128)(2,1)S(1)}, bf16[512,128]{1,0:T(8,128)(2,1)S(1)}, u32[]{:S(2)}, u32[]{:S(2)}) collective-permute-start(bf16[512,128]{1,0:T(8,128)(2,1)S(1)} %get-tuple-element.81), channel_id=1, source_target_pairs={{0,3},{1,2},{2,1},{3,0},{4,7},{5,6},{6,5},{7,4},{8,11},{9,10},{10,... | collective-permute-start | bytes 393224 | tf_op jit(solution)/shard_map/ppermute | solution.py:453
  69.6 6.4 %collective-permute-start.24 = (bf16[512,128]{1,0:T(8,128)(2,1)S(1)}, bf16[512,128]{1,0:T(8,128)(2,1)S(1)}, u32[]{:S(2)}, u32[]{:S(2)}) collective-permute-start(bf16[512,128]{1,0:T(8,128)(2,1)S(1)} %get-tuple-element.82), channel_id=1, source_target_pairs={{0,4},{1,5},{2,6},{3,7},{4,0},{5,1},{6,2},{7,3},{8,12},{9,13},{10,... | collective-permute-start | bytes 393224 | tf_op jit(solution)/shard_map/ppermute | solution.py:453
  69.6 8.0 %collective-permute-start.25 = (bf16[512,128]{1,0:T(8,128)(2,1)S(1)}, bf16[512,128]{1,0:T(8,128)(2,1)S(1)}, u32[]{:S(2)}, u32[]{:S(2)}) collective-permute-start(bf16[512,128]{1,0:T(8,128)(2,1)S(1)} %get-tuple-element.83), channel_id=1, source_target_pairs={{0,5},{1,4},{2,7},{3,6},{4,1},{5,0},{6,3},{7,2},{8,13},{9,12},{10,... | collective-permute-start | bytes 393224 | tf_op jit(solution)/shard_map/ppermute | solution.py:453
  71.3 10.3 %collective-permute-start.20 = (bf16[512,128]{1,0:T(8,128)(2,1)S(1)}, bf16[512,128]{1,0:T(8,128)(2,1)S(1)}, u32[]{:S(2)}, u32[]{:S(2)}) collective-permute-start(bf16[512,128]{1,0:T(8,128)(2,1)S(1)} %get-tuple-element.77), channel_id=1, source_target_pairs={{0,6},{1,7},{2,4},{3,5},{4,2},{5,3},{6,0},{7,1},{8,14},{9,15},{10,... | collective-permute-start | bytes 393224 | tf_op jit(solution)/shard_map/ppermute | solution.py:453
  74.1 9.1 %collective-permute-start.19 = (bf16[512,128]{1,0:T(8,128)(2,1)S(1)}, bf16[512,128]{1,0:T(8,128)(2,1)S(1)}, u32[]{:S(2)}, u32[]{:S(2)}) collective-permute-start(bf16[512,128]{1,0:T(8,128)(2,1)S(1)} %get-tuple-element.76), channel_id=1, source_target_pairs={{0,7},{1,6},{2,5},{3,4},{4,3},{5,2},{6,1},{7,0},{8,15},{9,14},{10,... | collective-permute-start | bytes 393224 | tf_op jit(solution)/shard_map/ppermute | solution.py:453
  (5 other events, 16.1 us)
